TPU v7x, 128 devices: a whole 4x4x4 slice. The times are simulated.
128 devices in a mesh: grp: 16 (over z, y), rep: 8 (over x, core).
Axes of the slice: x: 4, y: 4, z: 4, core: 2. Of those that a mesh axis runs over, the one named last changes fastest.
Arguments:
- user_feats: bfloat16 [8, 4096, 256], P('rep', 'grp'), may hold values from -6 to 6
- tower_in: bfloat16 [256, 512], replicated, may hold values from -0.375 to 0.375
- tower_out: bfloat16 [512, 512], replicated, may hold values from -0.4375 to 0.4375
- table_a: bfloat16 [1048576, 256], P(('grp', 'rep')), may hold values from -6 to 6
- table_b: bfloat16 [1048576, 256], P(('grp', 'rep')), may hold values from -6 to 6
- ask_rows: int32 [16, 8, 16, 8, 16], P('grp', 'rep'), may hold values from 0 to 8191
- slot_src: int32 [16, 8, 2048], P('grp', 'rep'), may hold values from 0 to 2047
- slot_req: int32 [16, 8, 2048], P('grp', 'rep'), may hold values from 0 to 4095
- live_counts: int32 [8, 16], P('rep', 'grp'), may hold values from 1 to 2048, 16384 in all within a row
- cross_w: bfloat16 [3, 1024, 1024], replicated, may hold values from -0.09375 to 0.09375
- cross_b: float32 [3, 1024], replicated, may hold values from -3 to 3
- head_w: bfloat16 [1024], replicated, may hold values from -0.1875 to 0.1875
Outputs:
- logits: float32 [16, 8, 2048], P('grp', 'rep')
Inputs may be any that keep to these rules, and one draw needn't show every extreme that they name: `ask_rows`: owner-local row ids. `live_counts`: for each index of rep the counts sum to 16384, and one device of it has all 2048 slots live.
All inputs are finite; a program needn't handle non-finite values.
Results may differ from a plain program's by a relative error of at most 0.013.
Values may be sent and summed in bfloat16 or wider, within the bound.
A program may use at most 128 MiB of HBM per device.

v0:
```python
import math

import jax
import jax.numpy as jnp
from jax import lax
from jax.sharding import PartitionSpec as P


def tower(feats, tower_in, tower_out):
    hidden = jax.nn.relu(jnp.dot(feats, tower_in, preferred_element_type=jnp.float32)).astype(
        jnp.bfloat16
    )
    return jnp.dot(hidden, tower_out, preferred_element_type=jnp.float32).astype(jnp.bfloat16)


def cross_stack(crossed_base, cross_w, cross_b, head_w):
    crossed = crossed_base
    base_wide = crossed_base.astype(jnp.float32)
    for layer_index in range(cross_w.shape[0]):
        mixed = (
            jnp.dot(crossed, cross_w[layer_index], preferred_element_type=jnp.float32)
            + cross_b[layer_index]
        )
        crossed = (base_wide * mixed + crossed.astype(jnp.float32)).astype(jnp.bfloat16)
    return jnp.dot(crossed, head_w, preferred_element_type=jnp.float32)


def select_rows(table, picks):
    count = picks.shape[0]
    block = math.gcd(count, 512)
    columns = jnp.arange(table.shape[0], dtype=jnp.int32)

    def one_block(block_picks):
        onehot = (block_picks[:, None] == columns[None, :]).astype(table.dtype)
        return jnp.dot(onehot, table, preferred_element_type=jnp.float32).astype(table.dtype)

    picked = lax.map(one_block, picks.reshape(count // block, block))
    return picked.reshape(count, table.shape[1])


def body(
    user_feats,
    tower_in,
    tower_out,
    table_a,
    table_b,
    ask_rows,
    slot_src,
    slot_req,
    live_counts,
    cross_w,
    cross_b,
    head_w,
):
    n_grp = lax.axis_size("grp")
    n_rep = lax.axis_size("rep")
    per_owner = ask_rows.shape[-1]
    row_width = 2 * table_a.shape[1]
    asks_flat = ask_rows[0, 0].reshape(n_grp * n_rep, per_owner)
    received_ids = lax.all_to_all(
        asks_flat, ("grp", "rep"), split_axis=0, concat_axis=0, tiled=True
    )
    returned = lax.all_to_all(
        jnp.concatenate(
            [jnp.take(table_a, received_ids, axis=0), jnp.take(table_b, received_ids, axis=0)],
            axis=-1,
        ),
        ("grp", "rep"),
        split_axis=0,
        concat_axis=0,
        tiled=True,
    )
    returned = returned.reshape(n_grp * n_rep * per_owner, row_width)
    own_vecs = tower(user_feats[0], tower_in, tower_out)
    group_vecs = lax.all_gather(own_vecs, "grp", axis=0, tiled=True)
    sources = slot_src[0, 0]
    requests = slot_req[0, 0]
    slot_count = sources.shape[0]
    item_rows = select_rows(returned, sources)
    user_rows = select_rows(group_vecs, requests)
    crossed_base = jnp.concatenate([user_rows, item_rows], axis=-1)
    scores = cross_stack(crossed_base, cross_w, cross_b, head_w)
    live_mask = jnp.arange(slot_count, dtype=jnp.int32) < live_counts[0, 0]
    scores = jnp.where(live_mask, scores, jnp.zeros_like(scores))
    return scores[None, None, :]


def solution(mesh):
    return jax.shard_map(
        body,
        mesh=mesh,
        in_specs=(
            P("rep", "grp", None),
            P(),
            P(),
            P(("grp", "rep"), None),
            P(("grp", "rep"), None),
            P("grp", "rep", None, None, None),
            P("grp", "rep", None),
            P("grp", "rep", None),
            P("rep", "grp"),
            P(),
            P(),
            P(),
        ),
        out_specs=P("grp", "rep", None),
        check_vma=False,
    )
```

profile of v0, /device:TPU:1, one launch (start us, length us, event | category | flops | bytes accessed | tf_op | source)
XLA Modules:
  0.0 162.8 jit_solution(3145646573427322553)
XLA Ops:
  6.5 0.0 copy-start
  6.5 0.0 all-gather.2.cloned.1.call-start
  6.5 1.0 copy-done
  7.6 2.2 %convolution_convert_fusion = bf16[256,512]{1,0:T(8,128)(2,1)} fusion(bf16[512,512]{1,0:T(8,128)(2,1)S(1)} %copy-done, bf16[256,512]{1,0:T(8,128)(2,1)} %param.19, bf16[1,256,256]{2,1,0:T(8,128)(2,1)} %param.18), kind=kOutput, calls=%fused_computation.39 | convolution fusion | flops 201719808 | bytes 1179648 | tf_op jit(solution)/shard_map/dot_general | solution.py:13
  9.7 0.0 all-gather.2.cloned.1.call-update
  9.8 21.0 %all_to_all.17 = s32[128,1,16]{2,1,0:T(1,128)S(1)} all-to-all(s32[128,1,16]{2,1,0:T(1,128)} %bitcast.70), channel_id=1, replica_groups=mesh['grp'=16,'rep'=8] {'grp','rep'}, dimensions={0} | all-to-all | bytes 16384 | tf_op jit(solution)/shard_map/all_to_all | solution.py:60
  30.8 0.1 reshape.46
  30.9 9.4 %gather_fusion = bf16[2048,256]{1,0:T(8,128)(2,1)S(1)} fusion(bf16[8192,256]{1,0:T(8,128)(2,1)} %param.21, s32[2048]{0:T(1024)S(1)} %broadcast_clamp_fusion), kind=kCustom, calls=%fused_computation.clone | custom fusion | bytes 2105344 | tf_op jit(solution)/shard_map/jit(_take)/gather | solution.py:65
  40.3 9.4 %gather_fusion.1 = bf16[2048,256]{1,0:T(8,128)(2,1)S(1)} fusion(bf16[8192,256]{1,0:T(8,128)(2,1)} %param.22, s32[2048]{0:T(1024)S(1)} %broadcast_clamp_fusion), kind=kCustom, calls=%fused_computation.1.clone | custom fusion | bytes 2105344 | tf_op jit(solution)/shard_map/jit(_take)/gather | solution.py:65
  49.7 0.5 broadcast_select_fusion.1
  50.2 0.0 copy-start.5
  50.2 0.0 copy-start.6
  50.2 0.0 copy-start.7
  50.2 0.0 copy-start.4
  50.2 1.6 pad_maximum_fusion.1
  51.8 4.6 %all-to-all-start.1 = ((bf16[128,16,512]{2,1,0:T(8,128)(2,1)}), bf16[128,16,512]{2,1,0:T(8,128)(2,1)S(1)}, u32[]{:S(2)}, u32[]{:S(2)}) async-start(bf16[128,16,512]{2,1,0:T(8,128)(2,1)} %pad_maximum_fusion.1), calls=%async_computation.1 | async-start | bytes 4194304 | tf_op jit(solution)/shard_map/all_to_all | solution.py:63
  56.4 0.6 broadcast.21
  57.0 0.0 copy-done.5
  57.0 0.7 reduce.6
  57.7 0.0 copy-done.6
  57.7 0.7 reduce.7
  58.4 0.0 copy-done.7
  59.1 0.0 copy-done.4
  59.1 29.8 %all-to-all-done.1 = bf16[128,16,512]{2,1,0:T(8,128)(2,1)S(1)} async-done(((bf16[128,16,512]{2,1,0:T(8,128)(2,1)}), bf16[128,16,512]{2,1,0:T(8,128)(2,1)S(1)}, u32[]{:S(2)}, u32[]{:S(2)}) %all-to-all-start.1) | async-done | bytes 2097184 | tf_op jit(solution)/shard_map/all_to_all | solution.py:63
  88.9 0.0 copy-start.3
  88.9 1.3 copy-done.3
  90.3 0.2 broadcast.8.clone
  90.4 11.7 %while.23 = (s32[]{:T(128)}, bf16[4,512,512]{2,1,0:T(8,128)(2,1)S(1)}, s32[4,512]{1,0:T(4,128)S(1)}, bf16[2048,512]{1,0:T(8,128)(2,1)}, s32[]{:T(128)}) while((s32[]{:T(128)}, bf16[4,512,512]{2,1,0:T(8,128)(2,1)S(1)}, s32[4,512]{1,0:T(4,128)S(1)}, bf16[2048,512]{1,0:T(8,128)(2,1)}, s32[]{:T(128)}) %tuple.49), condition=%wide.region_3.5_spmd.clone, body=%wide.region_2.4_spmd.clone.sunk | while | flops 1075052544 | bytes 2627653 | solution.py:37
  90.5 2.9 %fusion.57 = bf16[4,512,512]{2,1,0:T(8,128)(2,1)S(1)} fusion(bf16[4,512,512]{2,1,0:T(8,128)(2,1)S(1)} %get-tuple-element.159, s32[]{:T(128)} %get-tuple-element.158, bf16[2048,512]{1,0:T(8,128)(2,1)} %get-tuple-element.166, s32[512]{0:T(512)S(1)} %bitcast.71), kind=kOutput, calls=%fused_computation.16.clone.1 | convolution fusion | flops 1075052544 | bytes 2623492 | tf_op jit(solution)/shard_map/while/body/eval_jaxpr/dot_general | solution.py:35
  93.4 2.9 %fusion.57 = bf16[4,512,512]{2,1,0:T(8,128)(2,1)S(1)} fusion(bf16[4,512,512]{2,1,0:T(8,128)(2,1)S(1)} %get-tuple-element.159, s32[]{:T(128)} %get-tuple-element.158, bf16[2048,512]{1,0:T(8,128)(2,1)} %get-tuple-element.166, s32[512]{0:T(512)S(1)} %bitcast.71), kind=kOutput, calls=%fused_computation.16.clone.1 | convolution fusion | flops 1075052544 | bytes 2623492 | tf_op jit(solution)/shard_map/while/body/eval_jaxpr/dot_general | solution.py:35
  96.3 2.9 %fusion.57 = bf16[4,512,512]{2,1,0:T(8,128)(2,1)S(1)} fusion(bf16[4,512,512]{2,1,0:T(8,128)(2,1)S(1)} %get-tuple-element.159, s32[]{:T(128)} %get-tuple-element.158, bf16[2048,512]{1,0:T(8,128)(2,1)} %get-tuple-element.166, s32[512]{0:T(512)S(1)} %bitcast.71), kind=kOutput, calls=%fused_computation.16.clone.1 | convolution fusion | flops 1075052544 | bytes 2623492 | tf_op jit(solution)/shard_map/while/body/eval_jaxpr/dot_general | solution.py:35
  99.2 2.9 %fusion.57 = bf16[4,512,512]{2,1,0:T(8,128)(2,1)S(1)} fusion(bf16[4,512,512]{2,1,0:T(8,128)(2,1)S(1)} %get-tuple-element.159, s32[]{:T(128)} %get-tuple-element.158, bf16[2048,512]{1,0:T(8,128)(2,1)} %get-tuple-element.166, s32[512]{0:T(512)S(1)} %bitcast.71), kind=kOutput, calls=%fused_computation.16.clone.1 | convolution fusion | flops 1075052544 | bytes 2623492 | tf_op jit(solution)/shard_map/while/body/eval_jaxpr/dot_general | solution.py:35
  102.1 0.0 copy-start.1
  102.1 1.3 copy-done.1
  103.4 0.0 all-gather.2.cloned.1.call-done
  103.4 0.2 broadcast.8.clone.1
  103.6 18.4 %while.22 = (s32[]{:T(128)}, bf16[4,512,512]{2,1,0:T(8,128)(2,1)S(1)}, s32[4,512]{1,0:T(4,128)S(1)}, bf16[4096,512]{1,0:T(8,128)(2,1)}, s32[]{:T(128)}) while((s32[]{:T(128)}, bf16[4,512,512]{2,1,0:T(8,128)(2,1)S(1)}, s32[4,512]{1,0:T(4,128)S(1)}, bf16[4096,512]{1,0:T(8,128)(2,1)}, s32[]{:T(128)}) %tuple.44), condition=%wide.region_1.2_spmd.clone, body=%wide.region_0.1_spmd.clone.sunk | while | flops 2149842944 | bytes 4724805 | solution.py:37
  103.6 4.6 %fusion.55 = bf16[4,512,512]{2,1,0:T(8,128)(2,1)S(1)} fusion(bf16[4,512,512]{2,1,0:T(8,128)(2,1)S(1)} %get-tuple-element.174, s32[]{:T(128)} %get-tuple-element.173, bf16[4096,512]{1,0:T(8,128)(2,1)} %get-tuple-element.181, s32[512]{0:T(512)S(1)} %bitcast.72), kind=kOutput, calls=%fused_computation.9.clone.1 | convolution fusion | flops 2149842944 | bytes 4720644 | tf_op jit(solution)/shard_map/while/body/eval_jaxpr/dot_general | solution.py:35
  108.2 4.6 %fusion.55 = bf16[4,512,512]{2,1,0:T(8,128)(2,1)S(1)} fusion(bf16[4,512,512]{2,1,0:T(8,128)(2,1)S(1)} %get-tuple-element.174, s32[]{:T(128)} %get-tuple-element.173, bf16[4096,512]{1,0:T(8,128)(2,1)} %get-tuple-element.181, s32[512]{0:T(512)S(1)} %bitcast.72), kind=kOutput, calls=%fused_computation.9.clone.1 | convolution fusion | flops 2149842944 | bytes 4720644 | tf_op jit(solution)/shard_map/while/body/eval_jaxpr/dot_general | solution.py:35
  112.8 4.6 %fusion.55 = bf16[4,512,512]{2,1,0:T(8,128)(2,1)S(1)} fusion(bf16[4,512,512]{2,1,0:T(8,128)(2,1)S(1)} %get-tuple-element.174, s32[]{:T(128)} %get-tuple-element.173, bf16[4096,512]{1,0:T(8,128)(2,1)} %get-tuple-element.181, s32[512]{0:T(512)S(1)} %bitcast.72), kind=kOutput, calls=%fused_computation.9.clone.1 | convolution fusion | flops 2149842944 | bytes 4720644 | tf_op jit(solution)/shard_map/while/body/eval_jaxpr/dot_general | solution.py:35
  117.4 4.6 %fusion.55 = bf16[4,512,512]{2,1,0:T(8,128)(2,1)S(1)} fusion(bf16[4,512,512]{2,1,0:T(8,128)(2,1)S(1)} %get-tuple-element.174, s32[]{:T(128)} %get-tuple-element.173, bf16[4096,512]{1,0:T(8,128)(2,1)} %get-tuple-element.181, s32[512]{0:T(512)S(1)} %bitcast.72), kind=kOutput, calls=%fused_computation.9.clone.1 | convolution fusion | flops 2149842944 | bytes 4720644 | tf_op jit(solution)/shard_map/while/body/eval_jaxpr/dot_general | solution.py:35
  122.0 0.0 copy-start.2
  122.0 10.1 %fusion.25 = f32[2048,1024]{1,0:T(8,128)} fusion(bf16[3,1024,1024]{2,1,0:T(8,128)(2,1)} %param.27, bf16[2048,512]{1,0:T(8,128)(2,1)} %bitcast.64, bf16[2048,512]{1,0:T(8,128)(2,1)S(1)} %bitcast.61), kind=kOutput, calls=%fused_computation.33 | convolution fusion | flops 4303355904 | bytes 14680064 | tf_op jit(solution)/shard_map/dot_general | solution.py:21
  132.1 0.0 copy-done.2
  132.1 12.6 %fusion.16 = bf16[2048,1024]{1,0:T(8,128)(2,1)} fusion(f32[1024]{0:T(1024)S(1)} %bitcast.76, f32[2048,1024]{1,0:T(8,128)} %fusion.25, f32[1024]{0:T(1024)S(1)} %bitcast.75, bf16[3,1024,1024]{2,1,0:T(8,128)(2,1)} %param.27, bf16[2048,512]{1,0:T(8,128)(2,1)S(1)} %bitcast.66, bf16[2048,512]{1,0:T(8,128)(2,1)S(1)} %bitcast.62), kind=kOutput, calls=%fused_computation.24 | convolution fusion | flops 4339007488 | bytes 31469568 | tf_op jit(solution)/shard_map/dot_general | solution.py:21
  144.6 10.7 %fusion.19 = f32[1,2048]{1,0:T(1,128)S(1)} fusion(bf16[1024,1]{0,1:T(2,128)(2,1)S(1)} %reshape.54, bf16[2048,1024]{1,0:T(8,128)(2,1)} %fusion.16, f32[1024]{0:T(1024)S(1)} %bitcast.74, bf16[3,1024,1024]{2,1,0:T(8,128)(2,1)} %param.27, bf16[2048,512]{1,0:T(8,128)(2,1)} %bitcast.65, bf16[2048,512]{1,0:T(8,128)(2,1)S(1)} %bitcast.63), kind=kOutput, calls=%fused_computation.28 | convolution fusion | flops 4318035968 | bytes 14694400 | tf_op jit(solution)/shard_map/dot_general | solution.py:25
  155.3 0.6 fusion.38
  (15 shorter events, 0.1 us)
Async XLA Ops:
  6.5 1.0 copy-start
  6.5 96.9 %all-gather.2.cloned.1.call-start = ((), (), s32[]{:S(2)}) async-start(), calls=%async_computation.2 | async-start | bytes 4456448 | tf_op jit(solution)/shard_map/all_gather | solution.py:75
  50.2 6.8 %copy-start.5 = (s32[1,1,2048]{2,1,0:T(1,128)S(1)}, s32[1,1,2048]{2,1,0:T(1,128)}, u32[]{:S(2)}) copy-start(s32[1,1,2048]{2,1,0:T(1,128)} %param.24) | copy-start | bytes 24580
  50.2 7.5 %copy-start.6 = (s32[1,1,2048]{2,1,0:T(1,128)S(1)}, s32[1,1,2048]{2,1,0:T(1,128)}, u32[]{:S(2)}) copy-start(s32[1,1,2048]{2,1,0:T(1,128)} %param.25) | copy-start | bytes 24580
  50.2 8.2 %copy-start.7 = (bf16[1024]{0:T(1024)(128)(2,1)S(1)}, bf16[1024]{0:T(1024)(128)(2,1)}, u32[]{:S(2)}) copy-start(bf16[1024]{0:T(1024)(128)(2,1)} %param.29) | copy-start | bytes 6148
  50.2 8.9 %copy-start.4 = (f32[3,1024]{1,0:T(4,128)S(1)}, f32[3,1024]{1,0:T(4,128)}, u32[]{:S(2)}) copy-start(f32[3,1024]{1,0:T(4,128)} %param.28) | copy-start | bytes 36868
  51.8 37.1 %all-to-all-start.1 = ((bf16[128,16,512]{2,1,0:T(8,128)(2,1)}), bf16[128,16,512]{2,1,0:T(8,128)(2,1)S(1)}, u32[]{:S(2)}, u32[]{:S(2)}) async-start(bf16[128,16,512]{2,1,0:T(8,128)(2,1)} %pad_maximum_fusion.1), calls=%async_computation.1 | async-start | bytes 4194304 | tf_op jit(solution)/shard_map/all_to_all | solution.py:63
  88.9 1.3 copy-start.3
  102.1 1.3 copy-start.1
  122.0 10.1 %copy-start.2 = (bf16[4,512,512]{2,1,0:T(8,128)(2,1)S(1)}, bf16[4,512,512]{2,1,0:T(8,128)(2,1)}, u32[]{:S(2)}) copy-start(bf16[4,512,512]{2,1,0:T(8,128)(2,1)} %copy-done.1) | copy-start | bytes 6291460
Sparse Core Ops, SparseCore 0:
  9.9 75.9 all-gather.1
where the time goes:
time: 163 us
  matrix products  65.2 us (40%)
  waiting for transfers between devices  29.8 us (18%)
  local copies, waits for them, and re-layouts  23.5 us (14%)
  blocking collectives  21 us (13%)
  between operations  14.2 us (9%)
  starting transfers between devices  4.56 us (3%)
  other arithmetic  4.13 us (3%)
    all_to_all x1, waiting for transfers between devices, body(): lax.all_to_all(jnp.concatenate([jnp.take(table_a, received_ids, axis=0),...  29.8 us
    dot_general x8, matrix products, one_block(): jnp.dot(onehot, table, preferred_element_type=jnp.float32)  29.7 us
    dot_general x2, matrix products, cross_stack(): jnp.dot(crossed, cross_w[layer_index], preferred_element_type=jnp.float32)  22.7 us
    all_to_all x1, blocking collectives, body(): lax.all_to_all(asks_flat, ('grp', 'rep'), split_axis=0, concat_axis=0, ti...  21 us
    dot_general x1, matrix products, cross_stack(): return jnp.dot(crossed, head_w, preferred_element_type=jnp.float32)  10.7 us
    gather x1, local copies, waits for them, and re-layouts, body(): jnp.take(table_a, received_ids, axis=0)  9.39 us
    gather x1, local copies, waits for them, and re-layouts, body(): jnp.take(table_b, received_ids, axis=0)  9.37 us
    all_to_all x1, starting transfers between devices, body(): lax.all_to_all(jnp.concatenate([jnp.take(table_a, received_ids, axis=0),...  4.56 us
  transfers between devices with their start and end apart: 2, of which 1 were waited for; matrix products, arithmetic and copies ran while one was open for 21% of the time, Pallas kernels for 0%

commit v1 on v0

v1 whole, which is shorter than its diff:
```python
import math

import jax
import jax.numpy as jnp
from jax import lax
from jax.experimental import pallas as pl
from jax.experimental.pallas import tpu as pltpu
from jax.sharding import PartitionSpec as P

MESH = pl.DeviceIdType.MESH
DMA = pltpu.SemaphoreType.DMA
BF16 = jnp.bfloat16
F32 = jnp.float32

CAP = 16
STEPS = 128
CHUNK_STEPS = 16
CHUNKS = STEPS // CHUNK_STEPS
TABLE_CHUNKS = 8


def remote(src, dst, send, recv, device):
    return pltpu.make_async_remote_copy(
        src_ref=src, dst_ref=dst, send_sem=send, recv_sem=recv, device_id=device, device_id_type=MESH
    )


def step_shift(i):
    dc, j = i % 2, i // 2
    a, b, e = j % 4, (j // 4) % 4, j // 16
    return (a + b + e) % 4, (a + b) % 4, a, dc


def exchange_kernel(
    feats_ref, table_a_ref, table_b_ref, asks_ref, rows_out, feats_out,
    tables, stage, ids_half, ids_mine, ids_smem, send_rows, recv_rows, rows_wide, feats_all,
    table_sem, local_sem, ids_send, ids_recv, ag_send, ag_recv, row_send, row_recv,
):
    g, r = lax.axis_index("grp"), lax.axis_index("rep")
    z, y, x, c = g // 4, g % 4, r // 2, r % 2
    g_line = [(g + i) % 16 for i in range(16)]
    r_line = [(r + i) % 8 for i in range(8)]
    y_line = [z * 4 + (y + i) % 4 for i in range(4)]
    z_line = [((z + i) % 4) * 4 + y for i in range(4)]

    span = tables.shape[0] // TABLE_CHUNKS
    table_copies = []
    for k in range(TABLE_CHUNKS):
        for t, ref in enumerate((table_a_ref, table_b_ref)):
            table_copies.append(
                pltpu.make_async_copy(
                    ref.at[pl.ds(k * span, span)],
                    stage.at[t, pl.ds(k * span, span)],
                    table_sem.at[t, k],
                )
            )
    for copy in table_copies:
        copy.start()

    barrier = pltpu.get_barrier_semaphore()
    for i in range(1, 8):
        pl.semaphore_signal(barrier, inc=1, device_id=(g, r_line[i]), device_id_type=MESH)
    for i in range(1, 16):
        pl.semaphore_signal(barrier, inc=1, device_id=(g_line[i], r), device_id_type=MESH)
    own_feats = feats_all.at[0, 0], feats_all.at[1, 0]
    feats_all[0, 0] = feats_ref[0:128]
    feats_all[1, 0] = feats_ref[128:256]
    pl.semaphore_wait(barrier, 22)

    first = [remote(asks_ref.at[:, r_line[i]], ids_half.at[:, r], ids_send.at[0], ids_recv.at[0], (g, r_line[i])) for i in range(1, 8)]
    for copy in first:
        copy.start()
    own = pltpu.make_async_copy(asks_ref.at[:, r], ids_half.at[:, r], local_sem.at[0])
    own.start()
    for i in (1, 3, 2):
        remote(own_feats[0], feats_all.at[0, i], ag_send, ag_recv.at[0, i], (y_line[i], r)).start()
        remote(own_feats[1], feats_all.at[1, 4 * i], ag_send, ag_recv.at[1, i], (z_line[i], r)).start()
    for i in (1, 3, 2):
        remote(own_feats[0], feats_all.at[0, 4 * i], ag_send, ag_recv.at[0, 0], (z_line[i], r)).start()
        remote(own_feats[1], feats_all.at[1, i], ag_send, ag_recv.at[1, 0], (y_line[i], r)).start()
    own.wait()
    pltpu.make_async_copy(ids_half.at[:, pl.ds(0, 7)], ids_half.at[:, pl.ds(0, 7)], ids_recv.at[0]).wait()
    for i in range(1, 16):
        remote(ids_half.at[g_line[i]], ids_mine.at[g], ids_send.at[1], ids_recv.at[1], (g_line[i], r)).start()
    own = pltpu.make_async_copy(ids_half.at[g], ids_mine.at[g], local_sem.at[0])
    own.start()
    for j in (1, 3, 2):
        remote(own_feats[0], feats_all.at[0, j], ag_send, ag_recv.at[0, j], (y_line[j], r)).wait_recv()
        for i in (1, 3, 2):
            remote(feats_all.at[0, j], feats_all.at[0, 4 * i + j], ag_send, ag_recv.at[0, 0], (z_line[i], r)).start()
        remote(own_feats[1], feats_all.at[1, 4 * j], ag_send, ag_recv.at[1, j], (z_line[j], r)).wait_recv()
        for i in (1, 3, 2):
            remote(feats_all.at[1, 4 * j], feats_all.at[1, 4 * j + i], ag_send, ag_recv.at[1, 0], (y_line[i], r)).start()

    for k in range(TABLE_CHUNKS):
        for t in range(2):
            table_copies[2 * k + t].wait()

        @pl.loop(0, span // 64)
        def _(j):
            at = pl.multiple_of(k * span + j * 64, 64)
            tables[pl.ds(at, 64), 0:256] = stage[0, pl.ds(at, 64), :].astype(F32)
            tables[pl.ds(at, 64), 256:512] = stage[1, pl.ds(at, 64), :].astype(F32)

    own.wait()
    pltpu.make_async_copy(ids_half.at[pl.ds(0, 15)], ids_mine.at[pl.ds(0, 15)], ids_recv.at[1]).wait()
    to_smem = pltpu.make_async_copy(ids_mine, ids_smem, local_sem.at[1])
    to_smem.start()
    to_smem.wait()

    def gathered(buffer, to_g, to_r):
        for k in range(CAP):
            row = ids_smem[to_g, to_r, 0, k]
            rows_wide[buffer, pl.ds(k, 1), :] = tables[pl.ds(row, 1), :]
        return rows_wide[buffer].astype(BF16)

    recv_rows[0] = gathered(0, g, r)

    def send_step(i, buffer):
        dz, dy, dx, dc = step_shift(i)
        to_g = ((z + dz) % 4) * 4 + (y + dy) % 4
        to_r = ((x + dx) % 4) * 2 + (c + dc) % 2
        send_rows[i] = gathered(buffer, to_g, to_r)
        remote(send_rows.at[i], recv_rows.at[i], row_send, row_recv.at[i // CHUNK_STEPS], (to_g, to_r)).start()

    send_step(1, 1)

    @pl.loop(1, STEPS // 2)
    def _(j):
        send_step(2 * j, 0)
        send_step(2 * j + 1, 1)

    for h in range(2):
        pltpu.make_async_copy(feats_all.at[h, pl.ds(0, 12)], feats_all.at[h, pl.ds(4, 12)], ag_recv.at[h, 0]).wait()
    for k in range(CHUNKS):
        n = CHUNK_STEPS - (k == 0)
        part = recv_rows.at[pl.ds(k * CHUNK_STEPS, n)]
        pltpu.make_async_copy(part, part, row_recv.at[k]).wait()
    rows_out[...] = recv_rows[...]
    feats_out[...] = feats_all[...]
    pltpu.make_async_copy(ids_half.at[:, pl.ds(0, 7)], ids_half.at[:, pl.ds(0, 7)], ids_send.at[0]).wait()
    pltpu.make_async_copy(ids_half.at[pl.ds(0, 15)], ids_mine.at[pl.ds(0, 15)], ids_send.at[1]).wait()
    for h in range(2):
        pltpu.make_async_copy(feats_all.at[h, pl.ds(0, 15)], feats_all.at[h, pl.ds(1, 15)], ag_send).wait()
    part = send_rows.at[pl.ds(0, STEPS - 1)]
    pltpu.make_async_copy(part, part, row_send).wait()


def exchange(feats, table_a, table_b, asks):
    vmem = pl.BlockSpec(memory_space=pltpu.VMEM)
    anywhere = pl.BlockSpec(memory_space=pl.ANY)
    rows_dev, e = table_a.shape
    return pl.pallas_call(
        exchange_kernel,
        out_shape=[
            jax.ShapeDtypeStruct((STEPS, CAP, 2 * e), BF16),
            jax.ShapeDtypeStruct((2, 16, 128, 256), BF16),
        ],
        in_specs=[vmem, anywhere, anywhere, vmem],
        out_specs=[vmem, vmem],
        scratch_shapes=[
            pltpu.VMEM((rows_dev, 2 * e), F32),
            pltpu.VMEM((2, rows_dev, e), BF16),
            pltpu.VMEM((16, 8, 1, CAP), jnp.int32),
            pltpu.VMEM((16, 8, 1, CAP), jnp.int32),
            pltpu.SMEM((16, 8, 1, CAP), jnp.int32),
            pltpu.VMEM((STEPS, CAP, 2 * e), BF16),
            pltpu.VMEM((STEPS, CAP, 2 * e), BF16),
            pltpu.VMEM((2, CAP, 2 * e), F32),
            pltpu.VMEM((2, 16, 128, 256), BF16),
            DMA((2, TABLE_CHUNKS)),
            DMA((2,)),
            DMA((2,)),
            DMA((2,)),
            DMA,
            DMA((2, 4)),
            DMA,
            DMA((CHUNKS,)),
        ],
        compiler_params=pltpu.CompilerParams(
            collective_id=0, has_side_effects=True, vmem_limit_bytes=52 * 1024 * 1024
        ),
    )(feats, table_a, table_b, asks)


def tower(feats, tower_in, tower_out):
    hidden = jax.nn.relu(jnp.dot(feats, tower_in, preferred_element_type=F32)).astype(BF16)
    return jnp.dot(hidden, tower_out, preferred_element_type=F32).astype(BF16)


def cross_stack(crossed_base, cross_w, cross_b, head_w):
    crossed = crossed_base
    base_wide = crossed_base.astype(F32)
    for layer_index in range(cross_w.shape[0]):
        mixed = jnp.dot(crossed, cross_w[layer_index], preferred_element_type=F32) + cross_b[layer_index]
        crossed = (base_wide * mixed + crossed.astype(F32)).astype(BF16)
    return jnp.dot(crossed, head_w, preferred_element_type=F32)


def select_rows(table, picks):
    count = picks.shape[0]
    block = math.gcd(count, 512)
    columns = jnp.arange(table.shape[0], dtype=jnp.int32)

    def one_block(block_picks):
        onehot = (block_picks[:, None] == columns[None, :]).astype(table.dtype)
        return jnp.dot(onehot, table, preferred_element_type=F32).astype(table.dtype)

    picked = lax.map(one_block, picks.reshape(count // block, block))
    return picked.reshape(count, table.shape[1])


def item_places(sources):
    g, r = lax.axis_index("grp"), lax.axis_index("rep")
    z, y, x, c = g // 4, g % 4, r // 2, r % 2
    owner, k = sources // CAP, sources % CAP
    og, o_r = owner // 8, owner % 8
    dz, dy = (z - og // 4) % 4, (y - og % 4) % 4
    dx, dc = (x - o_r // 2) % 4, (c - o_r % 2) % 2
    a, b, e = dx, (dy - dx) % 4, (dz - dy) % 4
    return ((e * 16 + b * 4 + a) * 2 + dc) * CAP + k


def request_places(requests):
    g = lax.axis_index("grp")
    z, y = g // 4, g % 4
    og = requests // 256
    slot = ((z - og // 4) % 4) * 4 + (y - og % 4) % 4
    return (requests // 128) % 2 * 2048 + slot * 128 + requests % 128


def body(
    user_feats, tower_in, tower_out, table_a, table_b, ask_rows, slot_src, slot_req, live_counts, cross_w, cross_b, head_w,
):
    rows, feats = exchange(user_feats[0], table_a, table_b, ask_rows.reshape(16, 8, 1, CAP))
    rows = rows.reshape(STEPS * CAP, rows.shape[-1])
    feats = feats.reshape(4096, feats.shape[-1])
    item_rows = select_rows(rows, item_places(slot_src[0, 0]))
    feat_rows = select_rows(feats, request_places(slot_req[0, 0]))
    user_rows = tower(feat_rows, tower_in, tower_out)
    crossed_base = jnp.concatenate([user_rows, item_rows], axis=-1)
    scores = cross_stack(crossed_base, cross_w, cross_b, head_w)
    live_mask = jnp.arange(scores.shape[0], dtype=jnp.int32) < live_counts[0, 0]
    return jnp.where(live_mask, scores, jnp.zeros_like(scores))[None, None, :]


def solution(mesh):
    return jax.shard_map(
        body,
        mesh=mesh,
        in_specs=(
            P("rep", "grp", None), P(), P(),
            P(("grp", "rep"), None), P(("grp", "rep"), None),
            P("grp", "rep", None, None, None), P("grp", "rep", None), P("grp", "rep", None),
            P("rep", "grp"), P(), P(), P(),
        ),
        out_specs=P("grp", "rep", None),
        check_vma=False,
    )
```

time: 163 us -> 123 us (0.75)
  Pallas kernels: 0 us -> 50.9 us
  waiting for transfers between devices: 29.8 us -> 0 us
  blocking collectives: 21 us -> 0 us
  local copies, waits for them, and re-layouts: 23.5 us -> 5.36 us
  between operations: 14.2 us -> 0.75 us
  starting transfers between devices: 4.56 us -> 0 us
  matrix products: 65.2 us -> 61.9 us
    pallas_call x0 -> x1, Pallas kernels: none -> 50.9 us  [exchange(): pl.pallas_call(exchange_kernel, out_shape=[jax.ShapeDtypeStruct((STEPS, C...]
    all_to_all x1 -> x0, waiting for transfers between devices: 29.8 us -> none  [body(): lax.all_to_all(jnp.concatenate([jnp.take(table_a, received_ids, axis=0),...]
    all_to_all x1 -> x0, blocking collectives: 21 us -> none  [body(): lax.all_to_all(asks_flat, ('grp', 'rep'), split_axis=0, concat_axis=0, ti...]
    gather x2 -> x0, local copies, waits for them, and re-layouts: 18.8 us -> none  [the longest x1 9.39 us: body(): jnp.take(table_a, received_ids, axis=0)]
    all_to_all x1 -> x0, starting transfers between devices: 4.56 us -> none  [body(): lax.all_to_all(jnp.concatenate([jnp.take(table_a, received_ids, axis=0),...]
    dot_general x12, matrix products: 65.2 us -> 61.9 us  [the longest x8 23.8 us: one_block(): jnp.dot(onehot, table, preferred_element_type=F32).astype(table.dtype)]
    reshape x0 -> x1, local copies, waits for them, and re-layouts: none -> 2.92 us  [select_rows(): return picked.reshape(count, table.shape[1])]
    unnamed x18 -> x16, local copies, waits for them, and re-layouts: 4.29 us -> 2.36 us
  transfers between devices with their start and end apart: 2 -> 0, of which waited for: 1 -> 0; matrix products, arithmetic and copies ran while one was open for 21% -> 0% of each run, Pallas kernels for 0% -> 0%
where the time goes in v1:
time: 123 us
  matrix products  61.9 us (50%)
  Pallas kernels  50.9 us (41%)
  local copies, waits for them, and re-layouts  5.36 us (4%)
  other arithmetic  3.6 us (3%)
    pallas_call x1, Pallas kernels, exchange(): pl.pallas_call(exchange_kernel, out_shape=[jax.ShapeDtypeStruct((STEPS, C...  50.9 us
    dot_general x8, matrix products, one_block(): jnp.dot(onehot, table, preferred_element_type=F32).astype(table.dtype)  23.8 us
    dot_general x2, matrix products, cross_stack(): jnp.dot(crossed, cross_w[layer_index], preferred_element_type=F32)  23.2 us
    dot_general x1, matrix products, cross_stack(): return jnp.dot(crossed, head_w, preferred_element_type=F32)  10.6 us
    dot_general x1, matrix products, tower(): return jnp.dot(hidden, tower_out, preferred_element_type=F32).astype(BF16)  4.35 us
    reshape x1, local copies, waits for them, and re-layouts, select_rows(): return picked.reshape(count, table.shape[1])  2.92 us
    unnamed x2, other arithmetic  2.82 us

profile of v1, /device:TPU:1, one launch (start us, length us, event | category | flops | bytes accessed | tf_op | source)
XLA Modules:
  0.0 122.5 jit_solution(11548610150600522008)
XLA Ops:
  0.0 0.0 copy-start
  0.0 0.6 broadcast.222
  0.6 1.4 %reduce.7 = s32[2048]{0:T(1024)S(1)} reduce(s32[1,1,2048]{2,1,0:T(1,128)} %param.23, s32[]{:T(128)} %broadcast.222), dimensions={0,1}, to_apply=%param.23.reduce_sub_computation.3 | reduce | bytes 16388 | tf_op args[7]
  2.0 1.4 %reduce.6 = s32[2048]{0:T(1024)S(1)} reduce(s32[1,1,2048]{2,1,0:T(1,128)} %param.22, s32[]{:T(128)} %broadcast.222), dimensions={0,1}, to_apply=%param.22.reduce_sub_computation.3 | reduce | bytes 16388 | tf_op args[6]
  3.4 0.2 fusion.37
  3.6 0.0 copy-start.1
  3.6 0.9 copy-done.1
  4.5 0.0 copy-start.2
  4.5 0.8 copy-done.2
  5.4 50.9 %shard_map.118 = (bf16[128,16,512]{2,1,0:T(8,128)(2,1)S(1)}, bf16[2,16,128,256]{3,2,1,0:T(8,128)(2,1)}) custom-call(bf16[256,256]{1,0:T(8,128)(2,1)S(1)} %bitcast.55, bf16[8192,256]{1,0:T(8,128)(2,1)} %table_a_ref.1, bf16[8192,256]{1,0:T(8,128)(2,1)} %table_b_ref.1, s32[16,8,1,16]{3,2,1,0:T(1,128)S(1)} %bitcast.56), custom_call_target="tpu_custom_call" | custom-call | tf_op jit(solution)/shard_map/pallas_call | solution.py:153
  56.2 8.4 %while.23 = (s32[]{:T(128)}, bf16[4,512,512]{2,1,0:T(8,128)(2,1)}, s32[4,512]{1,0:T(4,128)S(1)}, bf16[2048,512]{1,0:T(8,128)(2,1)S(1)}, s32[]{:T(128)}) while((s32[]{:T(128)}, bf16[4,512,512]{2,1,0:T(8,128)(2,1)}, s32[4,512]{1,0:T(4,128)S(1)}, bf16[2048,512]{1,0:T(8,128)(2,1)S(1)}, s32[]{:T(128)}) %tuple.47), condition=%wide.region_3.4_spmd.clone, body=%wide.region_2.3_spmd.clone.sunk | while | flops 1075052544 | bytes 2628161 | solution.py:209
  56.3 2.1 %fusion.90 = bf16[4,512,512]{2,1,0:T(8,128)(2,1)} fusion(bf16[4,512,512]{2,1,0:T(8,128)(2,1)} %get-tuple-element.162, s32[]{:T(128)} %get-tuple-element.161, bf16[2048,512]{1,0:T(8,128)(2,1)S(1)} %get-tuple-element.169, s32[512]{0:T(512)S(1)} %bitcast.58), kind=kOutput, calls=%fused_computation.14.clone.1 | convolution fusion | flops 1075052544 | bytes 2624000 | tf_op jit(solution)/shard_map/while/body/eval_jaxpr/dot_general | solution.py:207
  58.4 2.1 %fusion.90 = bf16[4,512,512]{2,1,0:T(8,128)(2,1)} fusion(bf16[4,512,512]{2,1,0:T(8,128)(2,1)} %get-tuple-element.162, s32[]{:T(128)} %get-tuple-element.161, bf16[2048,512]{1,0:T(8,128)(2,1)S(1)} %get-tuple-element.169, s32[512]{0:T(512)S(1)} %bitcast.58), kind=kOutput, calls=%fused_computation.14.clone.1 | convolution fusion | flops 1075052544 | bytes 2624000 | tf_op jit(solution)/shard_map/while/body/eval_jaxpr/dot_general | solution.py:207
  60.5 2.1 %fusion.90 = bf16[4,512,512]{2,1,0:T(8,128)(2,1)} fusion(bf16[4,512,512]{2,1,0:T(8,128)(2,1)} %get-tuple-element.162, s32[]{:T(128)} %get-tuple-element.161, bf16[2048,512]{1,0:T(8,128)(2,1)S(1)} %get-tuple-element.169, s32[512]{0:T(512)S(1)} %bitcast.58), kind=kOutput, calls=%fused_computation.14.clone.1 | convolution fusion | flops 1075052544 | bytes 2624000 | tf_op jit(solution)/shard_map/while/body/eval_jaxpr/dot_general | solution.py:207
  62.6 2.1 %fusion.90 = bf16[4,512,512]{2,1,0:T(8,128)(2,1)} fusion(bf16[4,512,512]{2,1,0:T(8,128)(2,1)} %get-tuple-element.162, s32[]{:T(128)} %get-tuple-element.161, bf16[2048,512]{1,0:T(8,128)(2,1)S(1)} %get-tuple-element.169, s32[512]{0:T(512)S(1)} %bitcast.58), kind=kOutput, calls=%fused_computation.14.clone.1 | convolution fusion | flops 1075052544 | bytes 2624000 | tf_op jit(solution)/shard_map/while/body/eval_jaxpr/dot_general | solution.py:207
  64.7 2.9 %copy.18 = bf16[2048,512]{0,1:T(8,128)(2,1)S(1)} copy(bf16[2048,512]{1,0:T(8,128)(2,1)} %bitcast.57) | data formatting | bytes 4194304 | tf_op jit(solution)/shard_map/reshape | solution.py:210
  67.6 0.0 copy-start.5
  67.6 15.4 %while.22 = (s32[]{:T(128)}, bf16[4,512,256]{2,1,0:T(8,128)(2,1)}, s32[4,512]{1,0:T(4,128)S(1)}, bf16[4096,256]{1,0:T(8,128)(2,1)}, s32[]{:T(128)}) while((s32[]{:T(128)}, bf16[4,512,256]{2,1,0:T(8,128)(2,1)}, s32[4,512]{1,0:T(4,128)S(1)}, bf16[4096,256]{1,0:T(8,128)(2,1)}, s32[]{:T(128)}) %tuple.46), condition=%wide.region_1.2_spmd.clone, body=%wide.region_0.1_spmd.clone.sunk | while | flops 1075970048 | bytes 2366017 | solution.py:209
  67.7 3.9 %fusion.88 = bf16[4,512,256]{2,1,0:T(8,128)(2,1)} fusion(bf16[4,512,256]{2,1,0:T(8,128)(2,1)} %get-tuple-element.177, s32[]{:T(128)} %get-tuple-element.176, bf16[4096,256]{1,0:T(8,128)(2,1)} %get-tuple-element.184, s32[512]{0:T(512)S(1)} %bitcast.59), kind=kOutput, calls=%fused_computation.7.clone.1 | convolution fusion | flops 1075970048 | bytes 2361856 | tf_op jit(solution)/shard_map/while/body/eval_jaxpr/dot_general | solution.py:207
  71.5 3.8 %fusion.88 = bf16[4,512,256]{2,1,0:T(8,128)(2,1)} fusion(bf16[4,512,256]{2,1,0:T(8,128)(2,1)} %get-tuple-element.177, s32[]{:T(128)} %get-tuple-element.176, bf16[4096,256]{1,0:T(8,128)(2,1)} %get-tuple-element.184, s32[512]{0:T(512)S(1)} %bitcast.59), kind=kOutput, calls=%fused_computation.7.clone.1 | convolution fusion | flops 1075970048 | bytes 2361856 | tf_op jit(solution)/shard_map/while/body/eval_jaxpr/dot_general | solution.py:207
  75.4 3.8 %fusion.88 = bf16[4,512,256]{2,1,0:T(8,128)(2,1)} fusion(bf16[4,512,256]{2,1,0:T(8,128)(2,1)} %get-tuple-element.177, s32[]{:T(128)} %get-tuple-element.176, bf16[4096,256]{1,0:T(8,128)(2,1)} %get-tuple-element.184, s32[512]{0:T(512)S(1)} %bitcast.59), kind=kOutput, calls=%fused_computation.7.clone.1 | convolution fusion | flops 1075970048 | bytes 2361856 | tf_op jit(solution)/shard_map/while/body/eval_jaxpr/dot_general | solution.py:207
  79.2 3.9 %fusion.88 = bf16[4,512,256]{2,1,0:T(8,128)(2,1)} fusion(bf16[4,512,256]{2,1,0:T(8,128)(2,1)} %get-tuple-element.177, s32[]{:T(128)} %get-tuple-element.176, bf16[4096,256]{1,0:T(8,128)(2,1)} %get-tuple-element.184, s32[512]{0:T(512)S(1)} %bitcast.59), kind=kOutput, calls=%fused_computation.7.clone.1 | convolution fusion | flops 1075970048 | bytes 2361856 | tf_op jit(solution)/shard_map/while/body/eval_jaxpr/dot_general | solution.py:207
  83.1 0.0 copy-done
  83.1 0.0 copy-done.5
  83.1 4.4 %convolution_convert_fusion = bf16[2048,512]{0,1:T(8,128)(2,1)} fusion(bf16[512,512]{1,0:T(8,128)(2,1)S(1)} %copy-done, bf16[2048,256]{1,0:T(8,128)(2,1)} %bitcast.66, bf16[256,512]{1,0:T(8,128)(2,1)S(1)} %copy-done.5), kind=kOutput, calls=%fused_computation.28 | convolution fusion | flops 1613758464 | bytes 3932160 | tf_op jit(solution)/shard_map/dot_general | solution.py:188
  87.4 0.0 copy-start.3
  87.4 0.0 copy-start.6
  87.4 10.2 %fusion.25 = f32[2048,1024]{0,1:T(8,128)} fusion(bf16[3,1024,1024]{2,1,0:T(8,128)(2,1)} %param.25, bf16[2048,512]{0,1:T(8,128)(2,1)S(1)} %copy.18, bf16[2048,512]{0,1:T(8,128)(2,1)} %convolution_convert_fusion), kind=kOutput, calls=%fused_computation.32 | convolution fusion | flops 4303355904 | bytes 14680064 | tf_op jit(solution)/shard_map/dot_general | solution.py:195
  97.7 0.0 copy-done.3
  97.7 0.0 copy-done.6
  97.7 0.0 copy-start.4
  97.7 13.0 %fusion.16 = bf16[2048,1024]{0,1:T(8,128)(2,1)} fusion(f32[1024]{0:T(1024)S(1)} %bitcast.63, f32[2048,1024]{0,1:T(8,128)} %fusion.25, f32[1024]{0:T(1024)S(1)} %bitcast.62, bf16[3,1024,1024]{2,1,0:T(8,128)(2,1)} %param.25, bf16[2048,512]{0,1:T(8,128)(2,1)S(1)} %copy.18, bf16[2048,512]{0,1:T(8,128)(2,1)S(1)} %copy-done.6), kind=kOutput, calls=%fused_computation.22 | convolution fusion | flops 4339007488 | bytes 31469568 | tf_op jit(solution)/shard_map/dot_general | solution.py:195
  110.7 0.0 copy-done.4
  110.7 10.6 %fusion.19 = f32[1,2048]{1,0:T(1,128)S(1)} fusion(bf16[1024,1]{0,1:T(2,128)(2,1)S(1)} %reshape.30, bf16[2048,1024]{0,1:T(8,128)(2,1)} %fusion.16, f32[1024]{0:T(1024)S(1)} %bitcast.61, bf16[3,1024,1024]{2,1,0:T(8,128)(2,1)} %param.25, bf16[2048,512]{0,1:T(8,128)(2,1)S(1)} %copy.18, bf16[2048,512]{0,1:T(8,128)(2,1)} %convolution_convert_fusion), kind=kOutput, calls=%fused_computation.27 | convolution fusion | flops 4318035968 | bytes 14694400 | tf_op jit(solution)/shard_map/dot_general | solution.py:197
  121.9 0.6 fusion.65
  (14 shorter events, 0.1 us)
Async XLA Ops:
  0.0 83.1 %copy-start = (bf16[512,512]{1,0:T(8,128)(2,1)S(1)}, bf16[512,512]{1,0:T(8,128)(2,1)}, u32[]{:S(2)}) copy-start(bf16[512,512]{1,0:T(8,128)(2,1)} %param.18) | copy-start | bytes 1572868
  3.6 0.9 copy-start.1
  4.5 0.8 copy-start.2
  67.6 15.5 %copy-start.5 = (bf16[256,512]{1,0:T(8,128)(2,1)S(1)}, bf16[256,512]{1,0:T(8,128)(2,1)}, u32[]{:S(2)}) copy-start(bf16[256,512]{1,0:T(8,128)(2,1)} %param.17) | copy-start | bytes 786436
  87.4 10.2 %copy-start.3 = (f32[3,1024]{1,0:T(4,128)S(1)}, f32[3,1024]{1,0:T(4,128)}, u32[]{:S(2)}) copy-start(f32[3,1024]{1,0:T(4,128)} %param.26) | copy-start | bytes 36868
  87.4 10.3 %copy-start.6 = (bf16[2048,512]{0,1:T(8,128)(2,1)S(1)}, bf16[2048,512]{0,1:T(8,128)(2,1)}, u32[]{:S(2)}) copy-start(bf16[2048,512]{0,1:T(8,128)(2,1)} %convolution_convert_fusion) | copy-start | bytes 6291460
  97.7 13.0 %copy-start.4 = (bf16[1024]{0:T(1024)(128)(2,1)S(1)}, bf16[1024]{0:T(1024)(128)(2,1)}, u32[]{:S(2)}) copy-start(bf16[1024]{0:T(1024)(128)(2,1)} %param.27) | copy-start | bytes 6148

commit v2 on v1

v2 whole, which is shorter than its diff:
```python
import jax
import jax.numpy as jnp
from jax import lax
from jax.experimental import pallas as pl
from jax.experimental.pallas import tpu as pltpu
from jax.sharding import PartitionSpec as P

MESH = pl.DeviceIdType.MESH
DMA = pltpu.SemaphoreType.DMA
BF16 = jnp.bfloat16
F32 = jnp.float32

CAP = 16
STEPS = 128
CHUNK_STEPS = 16
CHUNKS = STEPS // CHUNK_STEPS
TABLE_CHUNKS = 8
TILE = 512


def remote(src, dst, send, recv, device):
    return pltpu.make_async_remote_copy(
        src_ref=src, dst_ref=dst, send_sem=send, recv_sem=recv, device_id=device, device_id_type=MESH
    )


def step_shift(i):
    dc, j = i % 2, i // 2
    a, b, e = j % 4, (j // 4) % 4, j // 16
    return (a + b + e) % 4, (a + b) % 4, a, dc


def dot(a, b):
    return jnp.dot(a, b, preferred_element_type=F32)


def item_places(sources, z, y, x, c):
    owner, k = sources // CAP, sources % CAP
    og, o_r = owner // 8, owner % 8
    dz, dy = (z - og // 4 + 4) % 4, (y - og % 4 + 4) % 4
    dx, dc = (x - o_r // 2 + 4) % 4, (c - o_r % 2 + 2) % 2
    a, b, e = dx, (dy - dx + 4) % 4, (dz - dy + 4) % 4
    return ((e * 16 + b * 4 + a) * 2 + dc) * CAP + k


def request_places(requests, z, y):
    og = requests // 256
    slot = ((z - og // 4 + 4) % 4) * 4 + (y - og % 4 + 4) % 4
    return (requests // 128) % 2 * 2048 + slot * 128 + requests % 128


def to_columns(places, columns):
    wide = places.astype(F32)
    for k in range(places.shape[0]):
        row = jnp.broadcast_to(wide[k : k + 1, :], (128, 128))
        columns[128 * k : 128 * (k + 1), :] = row.T


def onehot(column, first, width):
    lanes = lax.broadcasted_iota(jnp.int32, (1, 128), 1).astype(F32)
    parts = [
        jnp.where(column == lanes + (first + 128 * k), 1.0, 0.0).astype(BF16) for k in range(width // 128)
    ]
    return jnp.concatenate(parts, axis=1)


def ranking_kernel(
    feats_ref, tower_in_ref, tower_out_ref, table_a_ref, table_b_ref, asks_ref, src_ref, req_ref, live_ref,
    cross_w_ref, cross_b_ref, head_ref, logits_ref,
    tables, stage, ids_half, ids_mine, ids_smem, send_rows, recv_rows, rows_wide, feats_all,
    cross_w, tower_in, tower_out, flipped, src_col, req_col, user, items,
    table_sem, weight_sem, local_sem, ids_send, ids_recv, ag_send, ag_recv, row_send, row_recv,
):
    g, r = lax.axis_index("grp"), lax.axis_index("rep")
    z, y, x, c = g // 4, g % 4, r // 2, r % 2
    g_line = [(g + i) % 16 for i in range(16)]
    r_line = [(r + i) % 8 for i in range(8)]
    y_line = [z * 4 + (y + i) % 4 for i in range(4)]
    z_line = [((z + i) % 4) * 4 + y for i in range(4)]

    span = tables.shape[0] // TABLE_CHUNKS
    table_copies = []
    for k in range(TABLE_CHUNKS):
        for t, ref in enumerate((table_a_ref, table_b_ref)):
            table_copies.append(
                pltpu.make_async_copy(
                    ref.at[pl.ds(k * span, span)],
                    stage.at[t, pl.ds(k * span, span)],
                    table_sem.at[t, k],
                )
            )
    for copy in table_copies:
        copy.start()
    weight_copies = [
        pltpu.make_async_copy(ref, scratch, weight_sem.at[n])
        for n, (ref, scratch) in enumerate(
            ((tower_in_ref, tower_in), (tower_out_ref, tower_out), (cross_w_ref, cross_w))
        )
    ]
    for copy in weight_copies:
        copy.start()

    barrier = pltpu.get_barrier_semaphore()
    for i in range(1, 8):
        pl.semaphore_signal(barrier, inc=1, device_id=(g, r_line[i]), device_id_type=MESH)
    for i in range(1, 16):
        pl.semaphore_signal(barrier, inc=1, device_id=(g_line[i], r), device_id_type=MESH)
    own_feats = feats_all.at[0], feats_all.at[16]
    feats_all[0] = feats_ref[0:128]
    feats_all[16] = feats_ref[128:256]
    pl.semaphore_wait(barrier, 22)

    first = [remote(asks_ref.at[:, r_line[i]], ids_half.at[:, r], ids_send.at[0], ids_recv.at[0], (g, r_line[i])) for i in range(1, 8)]
    for copy in first:
        copy.start()
    own = pltpu.make_async_copy(asks_ref.at[:, r], ids_half.at[:, r], local_sem.at[0])
    own.start()
    for i in (1, 3, 2):
        remote(own_feats[0], feats_all.at[i], ag_send, ag_recv.at[0, i], (y_line[i], r)).start()
        remote(own_feats[1], feats_all.at[16 + 4 * i], ag_send, ag_recv.at[1, i], (z_line[i], r)).start()
    for i in (1, 3, 2):
        remote(own_feats[0], feats_all.at[4 * i], ag_send, ag_recv.at[0, 0], (z_line[i], r)).start()
        remote(own_feats[1], feats_all.at[16 + i], ag_send, ag_recv.at[1, 0], (y_line[i], r)).start()
    own.wait()
    pltpu.make_async_copy(ids_half.at[:, pl.ds(0, 7)], ids_half.at[:, pl.ds(0, 7)], ids_recv.at[0]).wait()
    for i in range(1, 16):
        remote(ids_half.at[g_line[i]], ids_mine.at[g], ids_send.at[1], ids_recv.at[1], (g_line[i], r)).start()
    own = pltpu.make_async_copy(ids_half.at[g], ids_mine.at[g], local_sem.at[0])
    own.start()
    for j in (1, 3, 2):
        remote(own_feats[0], feats_all.at[j], ag_send, ag_recv.at[0, j], (y_line[j], r)).wait_recv()
        for i in (1, 3, 2):
            remote(feats_all.at[j], feats_all.at[4 * i + j], ag_send, ag_recv.at[0, 0], (z_line[i], r)).start()
        remote(own_feats[1], feats_all.at[16 + 4 * j], ag_send, ag_recv.at[1, j], (z_line[j], r)).wait_recv()
        for i in (1, 3, 2):
            remote(feats_all.at[16 + 4 * j], feats_all.at[16 + 4 * j + i], ag_send, ag_recv.at[1, 0], (y_line[i], r)).start()

    for k in range(TABLE_CHUNKS):
        for t in range(2):
            table_copies[2 * k + t].wait()

        @pl.loop(0, span // 64)
        def _(j):
            at = pl.multiple_of(k * span + j * 64, 64)
            tables[pl.ds(at, 64), 0:256] = stage[0, pl.ds(at, 64), :].astype(F32)
            tables[pl.ds(at, 64), 256:512] = stage[1, pl.ds(at, 64), :].astype(F32)

    own.wait()
    pltpu.make_async_copy(ids_half.at[pl.ds(0, 15)], ids_mine.at[pl.ds(0, 15)], ids_recv.at[1]).wait()
    to_smem = pltpu.make_async_copy(ids_mine, ids_smem, local_sem.at[1])
    to_smem.start()
    to_smem.wait()

    def gathered(buffer, to_g, to_r):
        for k in range(CAP):
            row = ids_smem[to_g, to_r, 0, k]
            rows_wide[buffer, pl.ds(k, 1), :] = tables[pl.ds(row, 1), :]
        return rows_wide[buffer].astype(BF16)

    recv_rows[0] = gathered(0, g, r)

    def send_step(i, buffer):
        dz, dy, dx, dc = step_shift(i)
        to_g = ((z + dz) % 4) * 4 + (y + dy) % 4
        to_r = ((x + dx) % 4) * 2 + (c + dc) % 2
        send_rows[i] = gathered(buffer, to_g, to_r)
        remote(send_rows.at[i], recv_rows.at[i], row_send, row_recv.at[i // CHUNK_STEPS], (to_g, to_r)).start()

    send_step(1, 1)

    @pl.loop(1, STEPS // 2)
    def _(j):
        send_step(2 * j, 0)
        send_step(2 * j + 1, 1)

    to_columns(item_places(src_ref[...], z, y, x, c), src_col)
    to_columns(request_places(req_ref[...], z, y), req_col)
    for copy in weight_copies:
        copy.wait()
    head = head_ref[...].astype(F32)
    flipped[...] = (cross_w[2].astype(F32) * head).T.astype(BF16)
    for h in range(2):
        pltpu.make_async_copy(
            feats_all.at[pl.ds(0, 12)], feats_all.at[pl.ds(0, 12)], ag_recv.at[h, 0]
        ).wait()
    slots, half = user.shape
    bias = cross_b_ref[...]

    @pl.loop(0, slots // TILE)
    def _(t):
        at = pl.ds(pl.multiple_of(t * TILE, TILE), TILE)
        column = req_col[at, :]
        picked = jnp.zeros((TILE, 256), F32)
        for k in range(4):
            picked += dot(onehot(column, 1024 * k, 1024), feats_all[8 * k : 8 * (k + 1)].reshape(1024, 256))
        hidden = jnp.maximum(dot(picked.astype(BF16), tower_in[...]), 0.0).astype(BF16)
        vec = dot(hidden, tower_out[...]).astype(BF16)
        user[at, :] = vec
        for n in range(2):
            cols = slice(half * n, half * (n + 1))
            mixed = dot(vec, cross_w[0, 0:half, cols]) + (bias[0:1, cols] + 1.0)
            turned = dot(vec, flipped[0:half, cols]) + head[:, cols]
            tables[pl.ds(pl.multiple_of(n * slots + t * TILE, TILE), TILE), :] = mixed
            tables[pl.ds(pl.multiple_of((n + 2) * slots + t * TILE, TILE), TILE), :] = turned

    for k in range(CHUNKS):
        n = CHUNK_STEPS - (k == 0)
        part = recv_rows.at[pl.ds(k * CHUNK_STEPS, n)]
        pltpu.make_async_copy(part, part, row_recv.at[k]).wait()
        width = CHUNK_STEPS * CAP

        @pl.loop(0, slots // TILE)
        def _(t):
            at = pl.ds(pl.multiple_of(t * TILE, TILE), TILE)
            rows = recv_rows[k * CHUNK_STEPS : (k + 1) * CHUNK_STEPS].reshape(width, half)
            picked = dot(onehot(src_col[at, :], k * width, width), rows)
            items[at, :] = picked if k == 0 else items[at, :] + picked

    live = live_ref[0, 0]
    by_bias = head * bias[2:3, :]

    @pl.loop(0, slots // TILE)
    def _(t):
        at = pl.ds(pl.multiple_of(t * TILE, TILE), TILE)
        item = items[at, :].astype(BF16)
        base = (user[at, :], item)
        crossed, turned = [], []
        for n in range(2):
            cols = slice(half * n, half * (n + 1))
            mixed = dot(item, cross_w[0, half:, cols]) + tables[pl.ds(pl.multiple_of(n * slots + t * TILE, TILE), TILE), :]
            crossed.append((base[n].astype(F32) * mixed).astype(BF16))
        crossed_1 = jnp.concatenate(crossed, axis=1)
        total = jnp.zeros((TILE, 128), F32)
        for n in range(2):
            cols = slice(half * n, half * (n + 1))
            wide = base[n].astype(F32)
            mixed = dot(crossed_1, cross_w[1, :, cols]) + bias[1:2, cols]
            crossed_2 = (wide * mixed + crossed[n].astype(F32)).astype(BF16).astype(F32)
            turned = dot(item, flipped[half:, cols]) + tables[pl.ds(pl.multiple_of((n + 2) * slots + t * TILE, TILE), TILE), :]
            score = crossed_2 * turned + wide * by_bias[:, cols]
            for m in range(half // 128):
                total += score[:, 128 * m : 128 * (m + 1)]
        for m in range(TILE // 128):
            scores = jnp.sum(total[128 * m : 128 * (m + 1), :].T, axis=0, keepdims=True)
            first = t * TILE + m * 128
            spots = lax.broadcasted_iota(jnp.int32, (1, 128), 1) + first
            logits_ref[pl.ds(t * (TILE // 128) + m, 1), :] = jnp.where(spots < live, scores, 0.0)

    pltpu.make_async_copy(ids_half.at[:, pl.ds(0, 7)], ids_half.at[:, pl.ds(0, 7)], ids_send.at[0]).wait()
    pltpu.make_async_copy(ids_half.at[pl.ds(0, 15)], ids_mine.at[pl.ds(0, 15)], ids_send.at[1]).wait()
    pltpu.make_async_copy(feats_all.at[pl.ds(0, 30)], feats_all.at[pl.ds(0, 30)], ag_send).wait()
    part = send_rows.at[pl.ds(0, STEPS - 1)]
    pltpu.make_async_copy(part, part, row_send).wait()


def body(
    user_feats, tower_in, tower_out, table_a, table_b, ask_rows, slot_src, slot_req, live_counts, cross_w, cross_b, head_w,
):
    vmem = pl.BlockSpec(memory_space=pltpu.VMEM)
    smem = pl.BlockSpec(memory_space=pltpu.SMEM)
    anywhere = pl.BlockSpec(memory_space=pl.ANY)
    rows_dev, e = table_a.shape
    slots = slot_src.shape[-1]
    x = cross_w.shape[-1]
    logits = pl.pallas_call(
        ranking_kernel,
        out_shape=jax.ShapeDtypeStruct((slots // 128, 128), F32),
        in_specs=[vmem, anywhere, anywhere, anywhere, anywhere, vmem, vmem, vmem, smem, anywhere, vmem, vmem],
        out_specs=vmem,
        scratch_shapes=[
            pltpu.VMEM((rows_dev, 2 * e), F32),
            pltpu.VMEM((2, rows_dev, e), BF16),
            pltpu.VMEM((16, 8, 1, CAP), jnp.int32),
            pltpu.VMEM((16, 8, 1, CAP), jnp.int32),
            pltpu.SMEM((16, 8, 1, CAP), jnp.int32),
            pltpu.VMEM((STEPS, CAP, 2 * e), BF16),
            pltpu.VMEM((STEPS, CAP, 2 * e), BF16),
            pltpu.VMEM((2, CAP, 2 * e), F32),
            pltpu.VMEM((32, 128, user_feats.shape[-1]), BF16),
            pltpu.VMEM(cross_w.shape, BF16),
            pltpu.VMEM(tower_in.shape, BF16),
            pltpu.VMEM(tower_out.shape, BF16),
            pltpu.VMEM((x, x), BF16),
            pltpu.VMEM((slots, 128), F32),
            pltpu.VMEM((slots, 128), F32),
            pltpu.VMEM((slots, x // 2), BF16),
            pltpu.VMEM((slots, x // 2), F32),
            DMA((2, TABLE_CHUNKS)),
            DMA((3,)),
            DMA((2,)),
            DMA((2,)),
            DMA((2,)),
            DMA,
            DMA((2, 4)),
            DMA,
            DMA((CHUNKS,)),
        ],
        compiler_params=pltpu.CompilerParams(
            collective_id=0, has_side_effects=True, vmem_limit_bytes=60 * 1024 * 1024
        ),
    )(
        user_feats[0], tower_in, tower_out, table_a, table_b, ask_rows.reshape(16, 8, 1, CAP),
        slot_src.reshape(slots // 128, 128), slot_req.reshape(slots // 128, 128), live_counts,
        cross_w, cross_b, head_w.reshape(1, x),
    )
    return logits.reshape(1, 1, slots)


def solution(mesh):
    return jax.shard_map(
        body,
        mesh=mesh,
        in_specs=(
            P("rep", "grp", None), P(), P(),
            P(("grp", "rep"), None), P(("grp", "rep"), None),
            P("grp", "rep", None, None, None), P("grp", "rep", None), P("grp", "rep", None),
            P("rep", "grp"), P(), P(), P(),
        ),
        out_specs=P("grp", "rep", None),
        check_vma=False,
    )
```

time: 123 us -> 87.2 us (0.71)
  the two profiles are of different devices: /device:TPU:1 before, /device:TPU:4 now
where the time goes in v2:
time: 87.2 us; the launch traced here: 87 us
  Pallas kernels  83.7 us (96%)
  local copies, waits for them, and re-layouts  2.57 us (3%)
    pallas_call x1, Pallas kernels, body(): pl.pallas_call(ranking_kernel, out_shape=jax.ShapeDtypeStruct((slots // 1...  83.7 us

profile of v2, /device:TPU:4, one launch (start us, length us, event | category | flops | bytes accessed | tf_op | source)
XLA Modules:
  0.0 87.0 jit_solution(12003952163657573569)
XLA Ops:
  0.7 1.3 %reshape.18.head_ref = bf16[1,1024]{1,0:T(2,128)(2,1)} reshape(bf16[1024]{0:T(1024)(128)(2,1)} %param.23) | data formatting | bytes 4096 | tf_op jit(solution)/shard_map/reshape | solution.py:304
  1.9 83.7 %shard_map.118 = f32[16,128]{1,0:T(8,128)} custom-call(bf16[256,256]{1,0:T(8,128)(2,1)} %bitcast.5, bf16[256,512]{1,0:T(8,128)(2,1)} %tower_in_ref.1, bf16[512,512]{1,0:T(8,128)(2,1)} %tower_out_ref.1, bf16[8192,256]{1,0:T(8,128)(2,1)} %table_a_ref.1, bf16[8192,256]{1,0:T(8,128)(2,1)} %table_b_ref.1, s32[16,8,1,16]{3,2,1,0:T(1,128)} %bitcast.6, ...), custom_call_target="tpu_custom_call" | custom-call | tf_op jit(solution)/shard_map/pallas_call | solution.py:265
  85.7 1.3 %copy.15 = f32[1,1,2048]{2,1,0:T(1,128)} copy(f32[1,1,2048]{2,1,0:T(1,128)} %bitcast.7) | data formatting | bytes 16384

commit v3 on v2

--- a/solution.py
+++ b/solution.py
@@ -12,22 +12,17 @@
 
 CAP = 16
 STEPS = 128
-CHUNK_STEPS = 16
-CHUNKS = STEPS // CHUNK_STEPS
+GROUP = 8
+PARTS = (0, 32, 64, 112, 128)
+CHUNKS = len(PARTS) - 1
 TABLE_CHUNKS = 8
-TILE = 512
+TILE = 1024
 
 
 def remote(src, dst, send, recv, device):
     return pltpu.make_async_remote_copy(
         src_ref=src, dst_ref=dst, send_sem=send, recv_sem=recv, device_id=device, device_id_type=MESH
     )
-
-
-def step_shift(i):
-    dc, j = i % 2, i // 2
-    a, b, e = j % 4, (j // 4) % 4, j // 16
-    return (a + b + e) % 4, (a + b) % 4, a, dc
 
 
 def dot(a, b):
@@ -65,7 +60,7 @@
 
 
 def ranking_kernel(
-    feats_ref, tower_in_ref, tower_out_ref, table_a_ref, table_b_ref, asks_ref, src_ref, req_ref, live_ref,
+    feats_ref, tower_in_ref, tower_out_ref, table_a_ref, table_b_ref, asks_ref, src_ref, req_ref,
     cross_w_ref, cross_b_ref, head_ref, logits_ref,
     tables, stage, ids_half, ids_mine, ids_smem, send_rows, recv_rows, rows_wide, feats_all,
     cross_w, tower_in, tower_out, flipped, src_col, req_col, user, items,
@@ -121,6 +116,16 @@
     for i in (1, 3, 2):
         remote(own_feats[0], feats_all.at[4 * i], ag_send, ag_recv.at[0, 0], (z_line[i], r)).start()
         remote(own_feats[1], feats_all.at[16 + i], ag_send, ag_recv.at[1, 0], (y_line[i], r)).start()
+    for k in range(TABLE_CHUNKS):
+        for t in range(2):
+            table_copies[2 * k + t].wait()
+
+        @pl.loop(0, span // 64)
+        def _(j):
+            at = pl.multiple_of(k * span + j * 64, 64)
+            tables[pl.ds(at, 64), 0:256] = stage[0, pl.ds(at, 64), :].astype(F32)
+            tables[pl.ds(at, 64), 256:512] = stage[1, pl.ds(at, 64), :].astype(F32)
+
     own.wait()
     pltpu.make_async_copy(ids_half.at[:, pl.ds(0, 7)], ids_half.at[:, pl.ds(0, 7)], ids_recv.at[0]).wait()
     for i in range(1, 16):
@@ -135,15 +140,14 @@
         for i in (1, 3, 2):
             remote(feats_all.at[16 + 4 * j], feats_all.at[16 + 4 * j + i], ag_send, ag_recv.at[1, 0], (y_line[i], r)).start()
 
-    for k in range(TABLE_CHUNKS):
-        for t in range(2):
-            table_copies[2 * k + t].wait()
-
-        @pl.loop(0, span // 64)
-        def _(j):
-            at = pl.multiple_of(k * span + j * 64, 64)
-            tables[pl.ds(at, 64), 0:256] = stage[0, pl.ds(at, 64), :].astype(F32)
-            tables[pl.ds(at, 64), 256:512] = stage[1, pl.ds(at, 64), :].astype(F32)
+    slots, half = user.shape
+    bias = cross_b_ref[...]
+    head = head_ref[...].astype(F32).reshape(1, 2 * half)
+    to_columns(item_places(src_ref[...], z, y, x, c), src_col)
+    to_columns(request_places(req_ref[...], z, y), req_col)
+    for copy in weight_copies:
+        copy.wait()
+    flipped[...] = (cross_w[2].astype(F32) * head).T.astype(BF16)
 
     own.wait()
     pltpu.make_async_copy(ids_half.at[pl.ds(0, 15)], ids_mine.at[pl.ds(0, 15)], ids_recv.at[1]).wait()
@@ -151,83 +155,92 @@
     to_smem.start()
     to_smem.wait()
 
-    def gathered(buffer, to_g, to_r):
-        for k in range(CAP):
-            row = ids_smem[to_g, to_r, 0, k]
-            rows_wide[buffer, pl.ds(k, 1), :] = tables[pl.ds(row, 1), :]
-        return rows_wide[buffer].astype(BF16)
-
-    recv_rows[0] = gathered(0, g, r)
-
-    def send_step(i, buffer):
-        dz, dy, dx, dc = step_shift(i)
-        to_g = ((z + dz) % 4) * 4 + (y + dy) % 4
-        to_r = ((x + dx) % 4) * 2 + (c + dc) % 2
-        send_rows[i] = gathered(buffer, to_g, to_r)
-        remote(send_rows.at[i], recv_rows.at[i], row_send, row_recv.at[i // CHUNK_STEPS], (to_g, to_r)).start()
-
-    send_step(1, 1)
-
-    @pl.loop(1, STEPS // 2)
+    r_hops = [((x + hop) % 4) * 2 + (c + dc) % 2 for hop in range(4) for dc in range(2)]
+
+    def partner(j, m):
+        hop_y = m // 2 + j % 4
+        hop_z = hop_y + j // 4
+        return ((z + hop_z) % 4) * 4 + (y + hop_y) % 4, r_hops[m]
+
+    @pl.loop(0, STEPS // GROUP)
     def _(j):
-        send_step(2 * j, 0)
-        send_step(2 * j + 1, 1)
-
-    to_columns(item_places(src_ref[...], z, y, x, c), src_col)
-    to_columns(request_places(req_ref[...], z, y), req_col)
-    for copy in weight_copies:
-        copy.wait()
-    head = head_ref[...].astype(F32)
-    flipped[...] = (cross_w[2].astype(F32) * head).T.astype(BF16)
+        for m in range(GROUP):
+            to_g, to_r = partner(j, m)
+            for k in range(CAP):
+                rows_wide[m % 2, pl.ds(k, 1), :] = tables[pl.ds(ids_smem[to_g, to_r, 0, k], 1), :]
+            send_rows[j * GROUP + m] = rows_wide[m % 2].astype(BF16)
+
+    recv_rows[0] = send_rows[0]
+
     for h in range(2):
         pltpu.make_async_copy(
             feats_all.at[pl.ds(0, 12)], feats_all.at[pl.ds(0, 12)], ag_recv.at[h, 0]
         ).wait()
-    slots, half = user.shape
-    bias = cross_b_ref[...]
+
+    def send_step(j, m, part):
+        i = j * GROUP + m
+        remote(send_rows.at[i], recv_rows.at[i], row_send, row_recv.at[part], partner(j, m)).start()
+
+    for m in range(1, GROUP):
+        send_step(0, m, 0)
+    for k in range(CHUNKS):
+
+        @pl.loop(max(PARTS[k] // GROUP, 1), PARTS[k + 1] // GROUP)
+        def _(j):
+            for m in range(GROUP):
+                send_step(j, m, k)
+
+    def arrived(k):
+        part = recv_rows.at[pl.ds(max(PARTS[k], 1), PARTS[k + 1] - max(PARTS[k], 1))]
+        pltpu.make_async_copy(part, part, row_recv.at[k]).wait()
+
+    def tile(t, first=0):
+        return pl.ds(pl.multiple_of(first + t * TILE, TILE), TILE)
+
+    def picked(t, k):
+        first, width = PARTS[k] * CAP, (PARTS[k + 1] - PARTS[k]) * CAP
+        rows = recv_rows[PARTS[k] : PARTS[k + 1]].reshape(width, half)
+        return dot(onehot(src_col[tile(t), :], first, width), rows)
+
+    def pick_part(k):
+        arrived(k)
+
+        @pl.loop(0, slots // TILE)
+        def _(t):
+            items[tile(t), :] = picked(t, k) if k == 0 else items[tile(t), :] + picked(t, k)
 
     @pl.loop(0, slots // TILE)
     def _(t):
-        at = pl.ds(pl.multiple_of(t * TILE, TILE), TILE)
-        column = req_col[at, :]
-        picked = jnp.zeros((TILE, 256), F32)
-        for k in range(4):
-            picked += dot(onehot(column, 1024 * k, 1024), feats_all[8 * k : 8 * (k + 1)].reshape(1024, 256))
-        hidden = jnp.maximum(dot(picked.astype(BF16), tower_in[...]), 0.0).astype(BF16)
-        vec = dot(hidden, tower_out[...]).astype(BF16)
-        user[at, :] = vec
+        places = onehot(req_col[tile(t), :], 0, 4096)
+        user[tile(t), 0:256] = dot(places, feats_all[...].reshape(4096, 256)).astype(BF16)
+
+    @pl.loop(0, slots // TILE)
+    def _(t):
+        hidden = jnp.maximum(dot(user[tile(t), 0:256], tower_in[...]), 0.0).astype(BF16)
+        user[tile(t), :] = dot(hidden, tower_out[...]).astype(BF16)
+
+    @pl.loop(0, slots // TILE)
+    def _(t):
+        vec = user[tile(t), :]
         for n in range(2):
             cols = slice(half * n, half * (n + 1))
-            mixed = dot(vec, cross_w[0, 0:half, cols]) + (bias[0:1, cols] + 1.0)
-            turned = dot(vec, flipped[0:half, cols]) + head[:, cols]
-            tables[pl.ds(pl.multiple_of(n * slots + t * TILE, TILE), TILE), :] = mixed
-            tables[pl.ds(pl.multiple_of((n + 2) * slots + t * TILE, TILE), TILE), :] = turned
-
-    for k in range(CHUNKS):
-        n = CHUNK_STEPS - (k == 0)
-        part = recv_rows.at[pl.ds(k * CHUNK_STEPS, n)]
-        pltpu.make_async_copy(part, part, row_recv.at[k]).wait()
-        width = CHUNK_STEPS * CAP
-
-        @pl.loop(0, slots // TILE)
-        def _(t):
-            at = pl.ds(pl.multiple_of(t * TILE, TILE), TILE)
-            rows = recv_rows[k * CHUNK_STEPS : (k + 1) * CHUNK_STEPS].reshape(width, half)
-            picked = dot(onehot(src_col[at, :], k * width, width), rows)
-            items[at, :] = picked if k == 0 else items[at, :] + picked
-
-    live = live_ref[0, 0]
+            tables[tile(t, n * slots), :] = dot(vec, cross_w[0, 0:half, cols]) + (bias[0:1, cols] + 1.0)
+            tables[tile(t, (n + 2) * slots), :] = dot(vec, flipped[0:half, cols]) + head[:, cols]
+
+    for k in range(CHUNKS - 1):
+        pick_part(k)
+    arrived(CHUNKS - 1)
+
     by_bias = head * bias[2:3, :]
 
     @pl.loop(0, slots // TILE)
     def _(t):
-        at = pl.ds(pl.multiple_of(t * TILE, TILE), TILE)
-        item = items[at, :].astype(BF16)
-        base = (user[at, :], item)
-        crossed, turned = [], []
+        item = (items[tile(t), :] + picked(t, CHUNKS - 1)).astype(BF16)
+        base = (user[tile(t), :], item)
+        crossed = []
         for n in range(2):
             cols = slice(half * n, half * (n + 1))
-            mixed = dot(item, cross_w[0, half:, cols]) + tables[pl.ds(pl.multiple_of(n * slots + t * TILE, TILE), TILE), :]
+            mixed = dot(item, cross_w[0, half:, cols]) + tables[tile(t, n * slots), :]
             crossed.append((base[n].astype(F32) * mixed).astype(BF16))
         crossed_1 = jnp.concatenate(crossed, axis=1)
         total = jnp.zeros((TILE, 128), F32)
@@ -236,15 +249,14 @@
             wide = base[n].astype(F32)
             mixed = dot(crossed_1, cross_w[1, :, cols]) + bias[1:2, cols]
             crossed_2 = (wide * mixed + crossed[n].astype(F32)).astype(BF16).astype(F32)
-            turned = dot(item, flipped[half:, cols]) + tables[pl.ds(pl.multiple_of((n + 2) * slots + t * TILE, TILE), TILE), :]
+            turned = dot(item, flipped[half:, cols]) + tables[tile(t, (n + 2) * slots), :]
             score = crossed_2 * turned + wide * by_bias[:, cols]
             for m in range(half // 128):
                 total += score[:, 128 * m : 128 * (m + 1)]
         for m in range(TILE // 128):
-            scores = jnp.sum(total[128 * m : 128 * (m + 1), :].T, axis=0, keepdims=True)
-            first = t * TILE + m * 128
-            spots = lax.broadcasted_iota(jnp.int32, (1, 128), 1) + first
-            logits_ref[pl.ds(t * (TILE // 128) + m, 1), :] = jnp.where(spots < live, scores, 0.0)
+            logits_ref[pl.ds(t * (TILE // 128) + m, 1), :] = jnp.sum(
+                total[128 * m : 128 * (m + 1), :].T, axis=0, keepdims=True
+            )
 
     pltpu.make_async_copy(ids_half.at[:, pl.ds(0, 7)], ids_half.at[:, pl.ds(0, 7)], ids_send.at[0]).wait()
     pltpu.make_async_copy(ids_half.at[pl.ds(0, 15)], ids_mine.at[pl.ds(0, 15)], ids_send.at[1]).wait()
@@ -257,7 +269,6 @@
     user_feats, tower_in, tower_out, table_a, table_b, ask_rows, slot_src, slot_req, live_counts, cross_w, cross_b, head_w,
 ):
     vmem = pl.BlockSpec(memory_space=pltpu.VMEM)
-    smem = pl.BlockSpec(memory_space=pltpu.SMEM)
     anywhere = pl.BlockSpec(memory_space=pl.ANY)
     rows_dev, e = table_a.shape
     slots = slot_src.shape[-1]
@@ -265,7 +276,7 @@
     logits = pl.pallas_call(
         ranking_kernel,
         out_shape=jax.ShapeDtypeStruct((slots // 128, 128), F32),
-        in_specs=[vmem, anywhere, anywhere, anywhere, anywhere, vmem, vmem, vmem, smem, anywhere, vmem, vmem],
+        in_specs=[vmem, anywhere, anywhere, anywhere, anywhere, vmem, vmem, vmem, anywhere, vmem, vmem],
         out_specs=vmem,
         scratch_shapes=[
             pltpu.VMEM((rows_dev, 2 * e), F32),
@@ -300,10 +311,11 @@
         ),
     )(
         user_feats[0], tower_in, tower_out, table_a, table_b, ask_rows.reshape(16, 8, 1, CAP),
-        slot_src.reshape(slots // 128, 128), slot_req.reshape(slots // 128, 128), live_counts,
-        cross_w, cross_b, head_w.reshape(1, x),
+        slot_src.reshape(slots // 128, 128), slot_req.reshape(slots // 128, 128),
+        cross_w, cross_b, head_w,
     )
-    return logits.reshape(1, 1, slots)
+    live = lax.broadcasted_iota(jnp.int32, (1, 1, slots), 2) < live_counts[0, 0]
+    return jnp.where(live, logits.reshape(1, 1, slots), 0.0)
 
 
 def solution(mesh):

time: 87.2 us -> 66.9 us (0.77)
  the two profiles are of different devices: /device:TPU:4 before, /device:TPU:1 now
where the time goes in v3:
time: 66.9 us; the launch traced here: 66.7 us
  Pallas kernels  64.8 us (97%)
  other arithmetic  1.31 us (2%)
    pallas_call x1, Pallas kernels, body(): pl.pallas_call(ranking_kernel, out_shape=jax.ShapeDtypeStruct((slots // 1...  64.8 us

profile of v3, /device:TPU:1, one launch (start us, length us, event | category | flops | bytes accessed | tf_op | source)
XLA Modules:
  0.0 66.7 jit_solution(15360855215052317375)
XLA Ops:
  0.7 64.8 %shard_map.118 = f32[16,128]{1,0:T(8,128)} custom-call(bf16[256,256]{1,0:T(8,128)(2,1)} %bitcast.7, bf16[256,512]{1,0:T(8,128)(2,1)} %tower_in_ref.1, bf16[512,512]{1,0:T(8,128)(2,1)} %tower_out_ref.1, bf16[8192,256]{1,0:T(8,128)(2,1)} %table_a_ref.1, bf16[8192,256]{1,0:T(8,128)(2,1)} %table_b_ref.1, s32[16,8,1,16]{3,2,1,0:T(1,128)} %bitcast.8, ...), custom_call_target="tpu_custom_call" | custom-call | tf_op jit(solution)/shard_map/pallas_call | solution.py:276
  65.4 1.3 %compare_select_fusion = f32[1,1,2048]{2,1,0:T(1,128)} fusion(f32[1,1,2048]{2,1,0:T(1,128)} %bitcast.9, s32[]{:T(128)} %bitcast.6), kind=kLoop, calls=%fused_computation | loop fusion | flops 4096 | bytes 16388 | tf_op jit(solution)/shard_map/jit(_where)/select_n | solution.py:318

commit v4 on v3

--- a/solution.py
+++ b/solution.py
@@ -13,6 +13,7 @@
 CAP = 16
 STEPS = 128
 GROUP = 8
+EARLY = 8
 PARTS = (0, 32, 64, 112, 128)
 CHUNKS = len(PARTS) - 1
 TABLE_CHUNKS = 8
@@ -62,9 +63,9 @@
 def ranking_kernel(
     feats_ref, tower_in_ref, tower_out_ref, table_a_ref, table_b_ref, asks_ref, src_ref, req_ref,
     cross_w_ref, cross_b_ref, head_ref, logits_ref,
-    tables, stage, ids_half, ids_mine, ids_smem, send_rows, recv_rows, rows_wide, feats_all,
+    src, req, cross_b, head_vmem, tables, stage, ids_half, ids_mine, ids_smem, send_rows, recv_rows, rows_wide, feats_all,
     cross_w, tower_in, tower_out, flipped, src_col, req_col, user, items,
-    table_sem, weight_sem, local_sem, ids_send, ids_recv, ag_send, ag_recv, row_send, row_recv,
+    small_sem, table_sem, weight_sem, local_sem, ids_send, ids_recv, ag_send, ag_recv, row_send, row_recv,
 ):
     g, r = lax.axis_index("grp"), lax.axis_index("rep")
     z, y, x, c = g // 4, g % 4, r // 2, r % 2
@@ -74,14 +75,34 @@
     z_line = [((z + i) % 4) * 4 + y for i in range(4)]
 
     span = tables.shape[0] // TABLE_CHUNKS
+    small_copies = [
+        pltpu.make_async_copy(ref, scratch, small_sem.at[n])
+        for n, (ref, scratch) in enumerate(
+            (
+                (feats_ref.at[0, pl.ds(0, 128)], feats_all.at[0]),
+                (feats_ref.at[0, pl.ds(128, 128)], feats_all.at[16]),
+                (src_ref, src),
+                (req_ref, req),
+                (cross_b_ref, cross_b),
+                (head_ref, head_vmem),
+            )
+        )
+    ]
+    for copy in small_copies:
+        copy.start()
+
+    barrier = pltpu.get_barrier_semaphore()
+    for i in range(1, 8):
+        pl.semaphore_signal(barrier, inc=1, device_id=(g, r_line[i]), device_id_type=MESH)
+    for i in range(1, 16):
+        pl.semaphore_signal(barrier, inc=1, device_id=(g_line[i], r), device_id_type=MESH)
+
     table_copies = []
     for k in range(TABLE_CHUNKS):
         for t, ref in enumerate((table_a_ref, table_b_ref)):
             table_copies.append(
                 pltpu.make_async_copy(
-                    ref.at[pl.ds(k * span, span)],
-                    stage.at[t, pl.ds(k * span, span)],
-                    table_sem.at[t, k],
+                    ref.at[pl.ds(k * span, span)], stage.at[t, pl.ds(k * span, span)], table_sem.at[t, k]
                 )
             )
     for copy in table_copies:
@@ -95,14 +116,8 @@
     for copy in weight_copies:
         copy.start()
 
-    barrier = pltpu.get_barrier_semaphore()
-    for i in range(1, 8):
-        pl.semaphore_signal(barrier, inc=1, device_id=(g, r_line[i]), device_id_type=MESH)
-    for i in range(1, 16):
-        pl.semaphore_signal(barrier, inc=1, device_id=(g_line[i], r), device_id_type=MESH)
-    own_feats = feats_all.at[0], feats_all.at[16]
-    feats_all[0] = feats_ref[0:128]
-    feats_all[16] = feats_ref[128:256]
+    for copy in small_copies:
+        copy.wait()
     pl.semaphore_wait(barrier, 22)
 
     first = [remote(asks_ref.at[:, r_line[i]], ids_half.at[:, r], ids_send.at[0], ids_recv.at[0], (g, r_line[i])) for i in range(1, 8)]
@@ -110,12 +125,29 @@
         copy.start()
     own = pltpu.make_async_copy(asks_ref.at[:, r], ids_half.at[:, r], local_sem.at[0])
     own.start()
-    for i in (1, 3, 2):
-        remote(own_feats[0], feats_all.at[i], ag_send, ag_recv.at[0, i], (y_line[i], r)).start()
-        remote(own_feats[1], feats_all.at[16 + 4 * i], ag_send, ag_recv.at[1, i], (z_line[i], r)).start()
-    for i in (1, 3, 2):
-        remote(own_feats[0], feats_all.at[4 * i], ag_send, ag_recv.at[0, 0], (z_line[i], r)).start()
-        remote(own_feats[1], feats_all.at[16 + i], ag_send, ag_recv.at[1, 0], (y_line[i], r)).start()
+    def block(h, first, second):
+        return 4 * second + first if h == 0 else 16 + 4 * first + second
+
+    def hand_on(h, at, to, leg, hop, part=None):
+        line = (y_line, z_line)[h if leg == 0 else 1 - h]
+        rows = pl.ds(0, 128) if part is None else pl.ds(64 * part, 64)
+        a, b = block(h, *at), block(h, *to)
+        remote(feats_all.at[a, rows], feats_all.at[b, rows], ag_send, ag_recv.at[b], (line[hop], r)).start()
+
+    def have(h, first, second):
+        part = feats_all.at[block(h, first, second)]
+        pltpu.make_async_copy(part, part, ag_recv.at[block(h, first, second)]).wait()
+
+    def to_both(h, first):
+        for hop in (1, 3):
+            hand_on(h, (first, 0), (first, hop), 1, hop)
+
+    for h in range(2):
+        for hop in (1, 3):
+            hand_on(h, (0, 0), (hop, 0), 0, hop)
+    for h in range(2):
+        to_both(h, 0)
+
     for k in range(TABLE_CHUNKS):
         for t in range(2):
             table_copies[2 * k + t].wait()
@@ -132,22 +164,33 @@
         remote(ids_half.at[g_line[i]], ids_mine.at[g], ids_send.at[1], ids_recv.at[1], (g_line[i], r)).start()
     own = pltpu.make_async_copy(ids_half.at[g], ids_mine.at[g], local_sem.at[0])
     own.start()
-    for j in (1, 3, 2):
-        remote(own_feats[0], feats_all.at[j], ag_send, ag_recv.at[0, j], (y_line[j], r)).wait_recv()
-        for i in (1, 3, 2):
-            remote(feats_all.at[j], feats_all.at[4 * i + j], ag_send, ag_recv.at[0, 0], (z_line[i], r)).start()
-        remote(own_feats[1], feats_all.at[16 + 4 * j], ag_send, ag_recv.at[1, j], (z_line[j], r)).wait_recv()
-        for i in (1, 3, 2):
-            remote(feats_all.at[16 + 4 * j], feats_all.at[16 + 4 * j + i], ag_send, ag_recv.at[1, 0], (y_line[i], r)).start()
+    for n, hop in enumerate((1, 3)):
+        for h in range(2):
+            have(h, hop, 0)
+            hand_on(h, (hop, 0), (2, 0), 0, hop, n)
+            to_both(h, hop)
+    for n, hop in enumerate((1, 3)):
+        for h in range(2):
+            have(h, 0, hop)
+            hand_on(h, (0, hop), (0, 2), 1, hop, n)
 
     slots, half = user.shape
-    bias = cross_b_ref[...]
-    head = head_ref[...].astype(F32).reshape(1, 2 * half)
-    to_columns(item_places(src_ref[...], z, y, x, c), src_col)
-    to_columns(request_places(req_ref[...], z, y), req_col)
+    bias = cross_b[...]
+    head = head_vmem[...].astype(F32).reshape(1, 2 * half)
+    to_columns(item_places(src[...], z, y, x, c), src_col)
+    to_columns(request_places(req[...], z, y), req_col)
     for copy in weight_copies:
         copy.wait()
     flipped[...] = (cross_w[2].astype(F32) * head).T.astype(BF16)
+
+    for h in range(2):
+        have(h, 2, 0)
+        to_both(h, 2)
+    for first in (1, 3):
+        for n, hop in enumerate((1, 3)):
+            for h in range(2):
+                have(h, first, hop)
+                hand_on(h, (first, hop), (first, 2), 1, hop, n)
 
     own.wait()
     pltpu.make_async_copy(ids_half.at[pl.ds(0, 15)], ids_mine.at[pl.ds(0, 15)], ids_recv.at[1]).wait()
@@ -162,33 +205,40 @@
         hop_z = hop_y + j // 4
         return ((z + hop_z) % 4) * 4 + (y + hop_y) % 4, r_hops[m]
 
-    @pl.loop(0, STEPS // GROUP)
-    def _(j):
+    def gather(j):
         for m in range(GROUP):
             to_g, to_r = partner(j, m)
             for k in range(CAP):
                 rows_wide[m % 2, pl.ds(k, 1), :] = tables[pl.ds(ids_smem[to_g, to_r, 0, k], 1), :]
             send_rows[j * GROUP + m] = rows_wide[m % 2].astype(BF16)
 
+    def send(j, k, first=0):
+        for m in range(first, GROUP):
+            i = j * GROUP + m
+            remote(send_rows.at[i], recv_rows.at[i], row_send, row_recv.at[k], partner(j, m)).start()
+
+    @pl.loop(0, EARLY)
+    def _(j):
+        gather(j)
+
+    for n, hop in enumerate((1, 3)):
+        for h in range(2):
+            have(h, 2, hop)
+            hand_on(h, (2, hop), (2, 2), 1, hop, n)
+
     recv_rows[0] = send_rows[0]
-
-    for h in range(2):
-        pltpu.make_async_copy(
-            feats_all.at[pl.ds(0, 12)], feats_all.at[pl.ds(0, 12)], ag_recv.at[h, 0]
-        ).wait()
-
-    def send_step(j, m, part):
-        i = j * GROUP + m
-        remote(send_rows.at[i], recv_rows.at[i], row_send, row_recv.at[part], partner(j, m)).start()
-
-    for m in range(1, GROUP):
-        send_step(0, m, 0)
+    send(0, 0, 1)
     for k in range(CHUNKS):
-
-        @pl.loop(max(PARTS[k] // GROUP, 1), PARTS[k + 1] // GROUP)
+        first, last = max(PARTS[k] // GROUP, 1), PARTS[k + 1] // GROUP
+
+        @pl.loop(first, min(max(EARLY, first), last))
         def _(j):
-            for m in range(GROUP):
-                send_step(j, m, k)
+            send(j, k)
+
+        @pl.loop(min(max(EARLY, first), last), last)
+        def _(j):
+            gather(j)
+            send(j, k)
 
     def arrived(k):
         part = recv_rows.at[pl.ds(max(PARTS[k], 1), PARTS[k + 1] - max(PARTS[k], 1))]
@@ -208,6 +258,10 @@
         @pl.loop(0, slots // TILE)
         def _(t):
             items[tile(t), :] = picked(t, k) if k == 0 else items[tile(t), :] + picked(t, k)
+
+    for first in range(4):
+        for h in range(2):
+            have(h, first, 2)
 
     @pl.loop(0, slots // TILE)
     def _(t):
@@ -276,9 +330,13 @@
     logits = pl.pallas_call(
         ranking_kernel,
         out_shape=jax.ShapeDtypeStruct((slots // 128, 128), F32),
-        in_specs=[vmem, anywhere, anywhere, anywhere, anywhere, vmem, vmem, vmem, anywhere, vmem, vmem],
+        in_specs=[anywhere] * 11,
         out_specs=vmem,
         scratch_shapes=[
+            pltpu.VMEM((slots // 128, 128), jnp.int32),
+            pltpu.VMEM((slots // 128, 128), jnp.int32),
+            pltpu.VMEM(cross_b.shape, F32),
+            pltpu.VMEM(head_w.shape, BF16),
             pltpu.VMEM((rows_dev, 2 * e), F32),
             pltpu.VMEM((2, rows_dev, e), BF16),
             pltpu.VMEM((16, 8, 1, CAP), jnp.int32),
@@ -296,13 +354,14 @@
             pltpu.VMEM((slots, 128), F32),
             pltpu.VMEM((slots, x // 2), BF16),
             pltpu.VMEM((slots, x // 2), F32),
+            DMA((6,)),
             DMA((2, TABLE_CHUNKS)),
             DMA((3,)),
             DMA((2,)),
             DMA((2,)),
             DMA((2,)),
             DMA,
-            DMA((2, 4)),
+            DMA((32,)),
             DMA,
             DMA((CHUNKS,)),
         ],
@@ -310,7 +369,7 @@
             collective_id=0, has_side_effects=True, vmem_limit_bytes=60 * 1024 * 1024
         ),
     )(
-        user_feats[0], tower_in, tower_out, table_a, table_b, ask_rows.reshape(16, 8, 1, CAP),
+        user_feats, tower_in, tower_out, table_a, table_b, ask_rows.reshape(16, 8, 1, CAP),
         slot_src.reshape(slots // 128, 128), slot_req.reshape(slots // 128, 128),
         cross_w, cross_b, head_w,
     )

time: 66.9 us -> 70.8 us (1.058)
  the two profiles are of different devices: /device:TPU:1 before, /device:TPU:26 now
where the time goes in v4:
time: 70.8 us; the launch traced here: 70.6 us
  Pallas kernels  68.7 us (97%)
  other arithmetic  1.31 us (2%)
    pallas_call x1, Pallas kernels, body(): pl.pallas_call(ranking_kernel, out_shape=jax.ShapeDtypeStruct((slots // 1...  68.7 us

profile of v4, /device:TPU:26, one launch (start us, length us, event | category | flops | bytes accessed | tf_op | source)
XLA Modules:
  0.0 70.6 jit_solution(403435247632983639)
XLA Ops:
  0.7 68.7 %shard_map.118 = f32[16,128]{1,0:T(8,128)} custom-call(bf16[1,256,256]{2,1,0:T(8,128)(2,1)} %feats_ref.1, bf16[256,512]{1,0:T(8,128)(2,1)} %tower_in_ref.1, bf16[512,512]{1,0:T(8,128)(2,1)} %tower_out_ref.1, bf16[8192,256]{1,0:T(8,128)(2,1)} %table_a_ref.1, bf16[8192,256]{1,0:T(8,128)(2,1)} %table_b_ref.1, s32[16,8,1,16]{3,2,1,0:T(1,128)} %bitcast.6, ...), custom_call_target="tpu_custom_call" | custom-call | tf_op jit(solution)/shard_map/pallas_call | solution.py:330
  69.3 1.3 %compare_select_fusion = f32[1,1,2048]{2,1,0:T(1,128)} fusion(f32[1,1,2048]{2,1,0:T(1,128)} %bitcast.7, s32[]{:T(128)} %bitcast.5), kind=kLoop, calls=%fused_computation | loop fusion | flops 4096 | bytes 16388 | tf_op jit(solution)/shard_map/jit(_where)/select_n | solution.py:377

commit v5 on v4

--- a/solution.py
+++ b/solution.py
@@ -13,8 +13,8 @@
 CAP = 16
 STEPS = 128
 GROUP = 8
-EARLY = 8
-PARTS = (0, 32, 64, 112, 128)
+EARLY = 3
+PARTS = (0, 48, 96, 112, 128)
 CHUNKS = len(PARTS) - 1
 TABLE_CHUNKS = 8
 TILE = 1024
@@ -179,9 +179,6 @@
     head = head_vmem[...].astype(F32).reshape(1, 2 * half)
     to_columns(item_places(src[...], z, y, x, c), src_col)
     to_columns(request_places(req[...], z, y), req_col)
-    for copy in weight_copies:
-        copy.wait()
-    flipped[...] = (cross_w[2].astype(F32) * head).T.astype(BF16)
 
     for h in range(2):
         have(h, 2, 0)
@@ -217,7 +214,7 @@
             i = j * GROUP + m
             remote(send_rows.at[i], recv_rows.at[i], row_send, row_recv.at[k], partner(j, m)).start()
 
-    @pl.loop(0, EARLY)
+    @pl.loop(0, 1)
     def _(j):
         gather(j)
 
@@ -226,6 +223,14 @@
             have(h, 2, hop)
             hand_on(h, (2, hop), (2, 2), 1, hop, n)
 
+    @pl.loop(1, EARLY)
+    def _(j):
+        gather(j)
+
+    for first in (0, 1, 3):
+        for h in range(2):
+            have(h, first, 2)
+
     recv_rows[0] = send_rows[0]
     send(0, 0, 1)
     for k in range(CHUNKS):
@@ -259,9 +264,12 @@
         def _(t):
             items[tile(t), :] = picked(t, k) if k == 0 else items[tile(t), :] + picked(t, k)
 
-    for first in range(4):
-        for h in range(2):
-            have(h, first, 2)
+    for copy in weight_copies:
+        copy.wait()
+    flipped[...] = (cross_w[2].astype(F32) * head).T.astype(BF16)
+
+    for h in range(2):
+        have(h, 2, 2)
 
     @pl.loop(0, slots // TILE)
     def _(t):

time: 70.8 us -> 63.7 us (0.90)
  the two profiles are of different devices: /device:TPU:26 before, /device:TPU:1 now
where the time goes in v5:
time: 63.7 us; the launch traced here: 62.7 us
  Pallas kernels  60.8 us (95%)
  other arithmetic  1.31 us (2%)
  between operations  0.66 us (1%)
    pallas_call x1, Pallas kernels, body(): pl.pallas_call(ranking_kernel, out_shape=jax.ShapeDtypeStruct((slots // 1...  60.8 us
    select_n x1, other arithmetic, body(): return jnp.where(live, logits.reshape(1, 1, slots), 0.0)  1.31 us

profile of v5, /device:TPU:1, one launch (start us, length us, event | category | flops | bytes accessed | tf_op | source)
XLA Modules:
  0.0 62.7 jit_solution(9067622105755092921)
XLA Ops:
  0.7 60.8 %shard_map.118 = f32[16,128]{1,0:T(8,128)} custom-call(bf16[1,256,256]{2,1,0:T(8,128)(2,1)} %feats_ref.1, bf16[256,512]{1,0:T(8,128)(2,1)} %tower_in_ref.1, bf16[512,512]{1,0:T(8,128)(2,1)} %tower_out_ref.1, bf16[8192,256]{1,0:T(8,128)(2,1)} %table_a_ref.1, bf16[8192,256]{1,0:T(8,128)(2,1)} %table_b_ref.1, s32[16,8,1,16]{3,2,1,0:T(1,128)} %bitcast.6, ...), custom_call_target="tpu_custom_call" | custom-call | tf_op jit(solution)/shard_map/pallas_call | solution.py:338
  61.4 1.3 %compare_select_fusion = f32[1,1,2048]{2,1,0:T(1,128)} fusion(f32[1,1,2048]{2,1,0:T(1,128)} %bitcast.7, s32[]{:T(128)} %bitcast.5), kind=kLoop, calls=%fused_computation | loop fusion | flops 4096 | bytes 16388 | tf_op jit(solution)/shard_map/jit(_where)/select_n | solution.py:385

commit v6 on v5

--- a/solution.py
+++ b/solution.py
@@ -14,7 +14,7 @@
 STEPS = 128
 GROUP = 8
 EARLY = 3
-PARTS = (0, 48, 96, 112, 128)
+PARTS = (0, 80, 112, 128)
 CHUNKS = len(PARTS) - 1
 TABLE_CHUNKS = 8
 TILE = 1024
@@ -64,7 +64,7 @@
     feats_ref, tower_in_ref, tower_out_ref, table_a_ref, table_b_ref, asks_ref, src_ref, req_ref,
     cross_w_ref, cross_b_ref, head_ref, logits_ref,
     src, req, cross_b, head_vmem, tables, stage, ids_half, ids_mine, ids_smem, send_rows, recv_rows, rows_wide, feats_all,
-    cross_w, tower_in, tower_out, flipped, src_col, req_col, user, items,
+    cross_w, tower_in, tower_out, flipped, src_col, req_smem, user, rows_a, items,
     small_sem, table_sem, weight_sem, local_sem, ids_send, ids_recv, ag_send, ag_recv, row_send, row_recv,
 ):
     g, r = lax.axis_index("grp"), lax.axis_index("rep")
@@ -175,10 +175,14 @@
             hand_on(h, (0, hop), (0, 2), 1, hop, n)
 
     slots, half = user.shape
+    width = half // 2
     bias = cross_b[...]
     head = head_vmem[...].astype(F32).reshape(1, 2 * half)
+    req[...] = request_places(req[...], z, y)
+    to_smem = pltpu.make_async_copy(req, req_smem, local_sem.at[1])
+    to_smem.start()
     to_columns(item_places(src[...], z, y, x, c), src_col)
-    to_columns(request_places(req[...], z, y), req_col)
+    to_smem.wait()
 
     for h in range(2):
         have(h, 2, 0)
@@ -206,13 +210,16 @@
         for m in range(GROUP):
             to_g, to_r = partner(j, m)
             for k in range(CAP):
-                rows_wide[m % 2, pl.ds(k, 1), :] = tables[pl.ds(ids_smem[to_g, to_r, 0, k], 1), :]
-            send_rows[j * GROUP + m] = rows_wide[m % 2].astype(BF16)
-
-    def send(j, k, first=0):
+                rows_wide[m, pl.ds(k, 1), :] = tables[pl.ds(ids_smem[to_g, to_r, 0, k], 1), :]
+            send_rows[j * GROUP + m] = rows_wide[m].astype(BF16)
+
+    def send(j, n, sem, first=0):
         for m in range(first, GROUP):
             i = j * GROUP + m
-            remote(send_rows.at[i], recv_rows.at[i], row_send, row_recv.at[k], partner(j, m)).start()
+            columns = pl.ds(n * width, width)
+            remote(
+                send_rows.at[i, :, columns], recv_rows.at[i, :, columns], row_send, row_recv.at[sem], partner(j, m)
+            ).start()
 
     @pl.loop(0, 1)
     def _(j):
@@ -232,33 +239,31 @@
             have(h, first, 2)
 
     recv_rows[0] = send_rows[0]
-    send(0, 0, 1)
-    for k in range(CHUNKS):
-        first, last = max(PARTS[k] // GROUP, 1), PARTS[k + 1] // GROUP
-
-        @pl.loop(first, min(max(EARLY, first), last))
-        def _(j):
-            send(j, k)
-
-        @pl.loop(min(max(EARLY, first), last), last)
-        def _(j):
-            gather(j)
-            send(j, k)
-
-    def arrived(k):
-        part = recv_rows.at[pl.ds(max(PARTS[k], 1), PARTS[k + 1] - max(PARTS[k], 1))]
-        pltpu.make_async_copy(part, part, row_recv.at[k]).wait()
+    send(0, 0, CHUNKS, 1)
+
+    @pl.loop(1, EARLY)
+    def _(j):
+        send(j, 0, CHUNKS)
+
+    @pl.loop(EARLY, STEPS // GROUP)
+    def _(j):
+        gather(j)
+        send(j, 0, CHUNKS)
+
+    def arrived(first, last, columns, sem):
+        part = recv_rows.at[pl.ds(max(first, 1), last - max(first, 1)), :, columns]
+        pltpu.make_async_copy(part, part, row_recv.at[sem]).wait()
 
     def tile(t, first=0):
         return pl.ds(pl.multiple_of(first + t * TILE, TILE), TILE)
 
     def picked(t, k):
-        first, width = PARTS[k] * CAP, (PARTS[k + 1] - PARTS[k]) * CAP
-        rows = recv_rows[PARTS[k] : PARTS[k + 1]].reshape(width, half)
-        return dot(onehot(src_col[tile(t), :], first, width), rows)
+        first, count = PARTS[k] * CAP, (PARTS[k + 1] - PARTS[k]) * CAP
+        rows = recv_rows[PARTS[k] : PARTS[k + 1], :, width:].reshape(count, width)
+        return dot(onehot(src_col[tile(t), :], first, count), rows)
 
     def pick_part(k):
-        arrived(k)
+        arrived(PARTS[k], PARTS[k + 1], pl.ds(width, width), k)
 
         @pl.loop(0, slots // TILE)
         def _(t):
@@ -271,38 +276,60 @@
     for h in range(2):
         have(h, 2, 2)
 
-    @pl.loop(0, slots // TILE)
-    def _(t):
-        places = onehot(req_col[tile(t), :], 0, 4096)
-        user[tile(t), 0:256] = dot(places, feats_all[...].reshape(4096, 256)).astype(BF16)
+    e = width
+
+    @pl.loop(0, 32)
+    def _(j):
+        tables[pl.ds(pl.multiple_of(128 * j, 128), 128), 0:e] = feats_all[j].astype(F32)
+
+    @pl.loop(0, slots // 128)
+    def _(j):
+        for m in range(8):
+            for k in range(16):
+                rows_wide[m, pl.ds(k, 1), 0:e] = tables[pl.ds(req_smem[j, 16 * m + k], 1), 0:e]
+            user[pl.ds(pl.multiple_of(128 * j, 128) + 16 * m, 16), 0:e] = rows_wide[m, :, 0:e].astype(BF16)
 
     @pl.loop(0, slots // TILE)
     def _(t):
         hidden = jnp.maximum(dot(user[tile(t), 0:256], tower_in[...]), 0.0).astype(BF16)
         user[tile(t), :] = dot(hidden, tower_out[...]).astype(BF16)
 
+    send(0, 1, 0, 1)
+    for k in range(CHUNKS):
+
+        @pl.loop(max(PARTS[k] // GROUP, 1), PARTS[k + 1] // GROUP)
+        def _(j):
+            send(j, 1, k)
+
+    arrived(0, STEPS, pl.ds(0, width), CHUNKS)
+
     @pl.loop(0, slots // TILE)
     def _(t):
-        vec = user[tile(t), :]
+        rows = recv_rows[:, :, 0:width].reshape(STEPS * CAP, width)
+        rows_a[tile(t), :] = dot(onehot(src_col[tile(t), :], 0, STEPS * CAP), rows).astype(BF16)
+
+    @pl.loop(0, slots // TILE)
+    def _(t):
+        early = jnp.concatenate([user[tile(t), :], rows_a[tile(t), :]], axis=1)
         for n in range(2):
             cols = slice(half * n, half * (n + 1))
-            tables[tile(t, n * slots), :] = dot(vec, cross_w[0, 0:half, cols]) + (bias[0:1, cols] + 1.0)
-            tables[tile(t, (n + 2) * slots), :] = dot(vec, flipped[0:half, cols]) + head[:, cols]
+            tables[tile(t, n * slots), :] = dot(early, cross_w[0, 0 : half + width, cols]) + (bias[0:1, cols] + 1.0)
+            tables[tile(t, (n + 2) * slots), :] = dot(early, flipped[0 : half + width, cols]) + head[:, cols]
 
     for k in range(CHUNKS - 1):
         pick_part(k)
-    arrived(CHUNKS - 1)
+    arrived(PARTS[-2], STEPS, pl.ds(width, width), CHUNKS - 1)
 
     by_bias = head * bias[2:3, :]
 
     @pl.loop(0, slots // TILE)
     def _(t):
         item = (items[tile(t), :] + picked(t, CHUNKS - 1)).astype(BF16)
-        base = (user[tile(t), :], item)
+        base = (user[tile(t), :], jnp.concatenate([rows_a[tile(t), :], item], axis=1))
         crossed = []
         for n in range(2):
             cols = slice(half * n, half * (n + 1))
-            mixed = dot(item, cross_w[0, half:, cols]) + tables[tile(t, n * slots), :]
+            mixed = dot(item, cross_w[0, half + width :, cols]) + tables[tile(t, n * slots), :]
             crossed.append((base[n].astype(F32) * mixed).astype(BF16))
         crossed_1 = jnp.concatenate(crossed, axis=1)
         total = jnp.zeros((TILE, 128), F32)
@@ -311,7 +338,7 @@
             wide = base[n].astype(F32)
             mixed = dot(crossed_1, cross_w[1, :, cols]) + bias[1:2, cols]
             crossed_2 = (wide * mixed + crossed[n].astype(F32)).astype(BF16).astype(F32)
-            turned = dot(item, flipped[half:, cols]) + tables[tile(t, (n + 2) * slots), :]
+            turned = dot(item, flipped[half + width :, cols]) + tables[tile(t, (n + 2) * slots), :]
             score = crossed_2 * turned + wide * by_bias[:, cols]
             for m in range(half // 128):
                 total += score[:, 128 * m : 128 * (m + 1)]
@@ -352,16 +379,17 @@
             pltpu.SMEM((16, 8, 1, CAP), jnp.int32),
             pltpu.VMEM((STEPS, CAP, 2 * e), BF16),
             pltpu.VMEM((STEPS, CAP, 2 * e), BF16),
-            pltpu.VMEM((2, CAP, 2 * e), F32),
+            pltpu.VMEM((GROUP, CAP, 2 * e), F32),
             pltpu.VMEM((32, 128, user_feats.shape[-1]), BF16),
             pltpu.VMEM(cross_w.shape, BF16),
             pltpu.VMEM(tower_in.shape, BF16),
             pltpu.VMEM(tower_out.shape, BF16),
             pltpu.VMEM((x, x), BF16),
             pltpu.VMEM((slots, 128), F32),
-            pltpu.VMEM((slots, 128), F32),
+            pltpu.SMEM((slots // 128, 128), jnp.int32),
             pltpu.VMEM((slots, x // 2), BF16),
-            pltpu.VMEM((slots, x // 2), F32),
+            pltpu.VMEM((slots, e), BF16),
+            pltpu.VMEM((slots, e), F32),
             DMA((6,)),
             DMA((2, TABLE_CHUNKS)),
             DMA((3,)),
@@ -371,7 +399,7 @@
             DMA,
             DMA((32,)),
             DMA,
-            DMA((CHUNKS,)),
+            DMA((CHUNKS + 1,)),
         ],
         compiler_params=pltpu.CompilerParams(
             collective_id=0, has_side_effects=True, vmem_limit_bytes=60 * 1024 * 1024

time: 63.7 us -> 64.1 us (level)
  the two profiles are of different devices: /device:TPU:1 before, /device:TPU:127 now
where the time goes in v6:
time: 64.1 us; the launch traced here: 63.9 us
  Pallas kernels  61.9 us (97%)
  other arithmetic  1.31 us (2%)
  between operations  0.66 us (1%)
    pallas_call x1, Pallas kernels, body(): pl.pallas_call(ranking_kernel, out_shape=jax.ShapeDtypeStruct((slots // 1...  61.9 us
    select_n x1, other arithmetic, body(): return jnp.where(live, logits.reshape(1, 1, slots), 0.0)  1.31 us

profile of v6, /device:TPU:127, one launch (start us, length us, event | category | flops | bytes accessed | tf_op | source)
XLA Modules:
  0.0 63.9 jit_solution(3328883300401933243)
XLA Ops:
  0.7 61.9 %shard_map.118 = f32[16,128]{1,0:T(8,128)} custom-call(bf16[1,256,256]{2,1,0:T(8,128)(2,1)} %feats_ref.1, bf16[256,512]{1,0:T(8,128)(2,1)} %tower_in_ref.1, bf16[512,512]{1,0:T(8,128)(2,1)} %tower_out_ref.1, bf16[8192,256]{1,0:T(8,128)(2,1)} %table_a_ref.1, bf16[8192,256]{1,0:T(8,128)(2,1)} %table_b_ref.1, s32[16,8,1,16]{3,2,1,0:T(1,128)} %bitcast.6, ...), custom_call_target="tpu_custom_call" | custom-call | tf_op jit(solution)/shard_map/pallas_call | solution.py:365
  62.6 1.3 %compare_select_fusion = f32[1,1,2048]{2,1,0:T(1,128)} fusion(f32[1,1,2048]{2,1,0:T(1,128)} %bitcast.7, s32[]{:T(128)} %bitcast.5), kind=kLoop, calls=%fused_computation | loop fusion | flops 4096 | bytes 16388 | tf_op jit(solution)/shard_map/jit(_where)/select_n | solution.py:413

commit v7 on v6

--- a/solution.py
+++ b/solution.py
@@ -301,6 +301,14 @@
         def _(j):
             send(j, 1, k)
 
+    @pl.loop(0, slots // TILE)
+    def _(t):
+        for n in range(2):
+            cols = slice(half * n, half * (n + 1))
+            vec = user[tile(t), :]
+            tables[tile(t, n * slots), :] = dot(vec, cross_w[0, 0:half, cols]) + (bias[0:1, cols] + 1.0)
+            tables[tile(t, (n + 2) * slots), :] = dot(vec, flipped[0:half, cols]) + head[:, cols]
+
     arrived(0, STEPS, pl.ds(0, width), CHUNKS)
 
     @pl.loop(0, slots // TILE)
@@ -310,11 +318,11 @@
 
     @pl.loop(0, slots // TILE)
     def _(t):
-        early = jnp.concatenate([user[tile(t), :], rows_a[tile(t), :]], axis=1)
+        vec = rows_a[tile(t), :]
         for n in range(2):
             cols = slice(half * n, half * (n + 1))
-            tables[tile(t, n * slots), :] = dot(early, cross_w[0, 0 : half + width, cols]) + (bias[0:1, cols] + 1.0)
-            tables[tile(t, (n + 2) * slots), :] = dot(early, flipped[0 : half + width, cols]) + head[:, cols]
+            tables[tile(t, n * slots), :] += dot(vec, cross_w[0, half : half + width, cols])
+            tables[tile(t, (n + 2) * slots), :] += dot(vec, flipped[half : half + width, cols])
 
     for k in range(CHUNKS - 1):
         pick_part(k)

time: 64.1 us -> 61.6 us (0.961)
  the two profiles are of different devices: /device:TPU:127 before, /device:TPU:1 now
where the time goes in v7:
time: 61.6 us; the launch traced here: 61.5 us
  Pallas kernels  59.5 us (97%)
  other arithmetic  1.31 us (2%)
  between operations  0.66 us (1%)
    pallas_call x1, Pallas kernels, body(): pl.pallas_call(ranking_kernel, out_shape=jax.ShapeDtypeStruct((slots // 1...  59.5 us
    select_n x1, other arithmetic, body(): return jnp.where(live, logits.reshape(1, 1, slots), 0.0)  1.31 us

profile of v7, /device:TPU:1, one launch (start us, length us, event | category | flops | bytes accessed | tf_op | source)
XLA Modules:
  0.0 61.5 jit_solution(16774558337851533125)
XLA Ops:
  0.7 59.5 %shard_map.118 = f32[16,128]{1,0:T(8,128)} custom-call(bf16[1,256,256]{2,1,0:T(8,128)(2,1)} %feats_ref.1, bf16[256,512]{1,0:T(8,128)(2,1)} %tower_in_ref.1, bf16[512,512]{1,0:T(8,128)(2,1)} %tower_out_ref.1, bf16[8192,256]{1,0:T(8,128)(2,1)} %table_a_ref.1, bf16[8192,256]{1,0:T(8,128)(2,1)} %table_b_ref.1, s32[16,8,1,16]{3,2,1,0:T(1,128)} %bitcast.6, ...), custom_call_target="tpu_custom_call" | custom-call | tf_op jit(solution)/shard_map/pallas_call | solution.py:373
  60.2 1.3 %compare_select_fusion = f32[1,1,2048]{2,1,0:T(1,128)} fusion(f32[1,1,2048]{2,1,0:T(1,128)} %bitcast.7, s32[]{:T(128)} %bitcast.5), kind=kLoop, calls=%fused_computation | loop fusion | flops 4096 | bytes 16388 | tf_op jit(solution)/shard_map/jit(_where)/select_n | solution.py:421

commit v8 on v7

--- a/solution.py
+++ b/solution.py
@@ -314,11 +314,8 @@
     @pl.loop(0, slots // TILE)
     def _(t):
         rows = recv_rows[:, :, 0:width].reshape(STEPS * CAP, width)
-        rows_a[tile(t), :] = dot(onehot(src_col[tile(t), :], 0, STEPS * CAP), rows).astype(BF16)
-
-    @pl.loop(0, slots // TILE)
-    def _(t):
-        vec = rows_a[tile(t), :]
+        vec = dot(onehot(src_col[tile(t), :], 0, STEPS * CAP), rows).astype(BF16)
+        rows_a[tile(t), :] = vec
         for n in range(2):
             cols = slice(half * n, half * (n + 1))
             tables[tile(t, n * slots), :] += dot(vec, cross_w[0, half : half + width, cols])
@@ -330,7 +327,7 @@
 
     by_bias = head * bias[2:3, :]
 
-    @pl.loop(0, slots // TILE)
+    @pl.loop(0, slots // TILE, unroll=2)
     def _(t):
         item = (items[tile(t), :] + picked(t, CHUNKS - 1)).astype(BF16)
         base = (user[tile(t), :], jnp.concatenate([rows_a[tile(t), :], item], axis=1))

time: 61.6 us -> 63.8 us (1.036)
  the two profiles are of different devices: /device:TPU:1 before, /device:TPU:82 now
where the time goes in v8:
time: 63.8 us; the launch traced here: 63.6 us
  Pallas kernels  61.7 us (97%)
  other arithmetic  1.31 us (2%)
  between operations  0.66 us (1%)
    pallas_call x1, Pallas kernels, body(): pl.pallas_call(ranking_kernel, out_shape=jax.ShapeDtypeStruct((slots // 1...  61.7 us
    select_n x1, other arithmetic, body(): return jnp.where(live, logits.reshape(1, 1, slots), 0.0)  1.31 us

profile of v8, /device:TPU:82, one launch (start us, length us, event | category | flops | bytes accessed | tf_op | source)
XLA Modules:
  0.0 63.6 jit_solution(5298603389957575756)
XLA Ops:
  0.7 61.7 %shard_map.118 = f32[16,128]{1,0:T(8,128)} custom-call(bf16[1,256,256]{2,1,0:T(8,128)(2,1)} %feats_ref.1, bf16[256,512]{1,0:T(8,128)(2,1)} %tower_in_ref.1, bf16[512,512]{1,0:T(8,128)(2,1)} %tower_out_ref.1, bf16[8192,256]{1,0:T(8,128)(2,1)} %table_a_ref.1, bf16[8192,256]{1,0:T(8,128)(2,1)} %table_b_ref.1, s32[16,8,1,16]{3,2,1,0:T(1,128)} %bitcast.6, ...), custom_call_target="tpu_custom_call" | custom-call | tf_op jit(solution)/shard_map/pallas_call | solution.py:370
  62.3 1.3 %compare_select_fusion = f32[1,1,2048]{2,1,0:T(1,128)} fusion(f32[1,1,2048]{2,1,0:T(1,128)} %bitcast.7, s32[]{:T(128)} %bitcast.5), kind=kLoop, calls=%fused_computation | loop fusion | flops 4096 | bytes 16388 | tf_op jit(solution)/shard_map/jit(_where)/select_n | solution.py:418
